TPU v7x, 32 devices: a whole 2x2x4 slice. The times are simulated.
32 devices in a mesh: dp: 8 (over z, x), mp: 4 (over y, core).
Axes of the slice: x: 2, y: 2, z: 4, core: 2. Of those that a mesh axis runs over, the one named last changes fastest.
Arguments:
- layer_input: bfloat16 [12288, 1024], P(('dp', 'mp')), may hold values from -6 to 6
- row_seq: int32 [12288], P(('dp', 'mp')), may hold values from -1 to 11, as said below
- qkv_weight: bfloat16 [1024, 3, 1024], P('dp', None, 'mp'), may hold values from -0.25 to 0.25
- out_weight: bfloat16 [1024, 1024], P('mp', 'dp'), may hold values from -0.75 to 0.75
- in_weight: bfloat16 [1024, 2, 2624], P('dp', None, 'mp'), may hold values from -0.1875 to 0.1875
- down_weight: bfloat16 [2624, 1024], P('mp', 'dp'), may hold values from -0.125 to 0.125
- attn_gain: bfloat16 [1024], P('dp'), may hold values from 0.099609375 to 1.8984375
- mlp_gain: bfloat16 [1024], P('dp'), may hold values from 0.099609375 to 1.8984375
- cotangent: bfloat16 [12288, 1024], P(('dp', 'mp')), may hold values from -6 to 6
Outputs:
- activations: bfloat16 [12288, 1024], P(('dp', 'mp'))
- input_grad: bfloat16 [12288, 1024], P(('dp', 'mp'))
- attn_gain_grad: float32 [1024], P('dp')
- mlp_gain_grad: float32 [1024], P('dp')
- qkv_grad: float32 [1024, 3, 1024], P('dp', None, 'mp')
- out_grad: float32 [1024, 1024], P('mp', 'dp')
- in_grad: float32 [1024, 2, 2624], P('dp', None, 'mp')
- down_grad: float32 [2624, 1024], P('mp', 'dp')
Inputs may be any that keep to these rules, and one draw needn't show every extreme that they name: `row_seq`: rows come in groups of 1536 (one index of dp, 12 blocks of 128 rows). In each group the sequence numbers rise from 0 without gaps, each sequence's rows are contiguous and start at a multiple of 128, a sequence has at most 1024 rows, padding (-1) stands only at the end of a sequence's last block and in whole blocks after a group's last sequence. Some group has sequences in all its blocks and begins with one of exactly 1024 rows; another group has a sequence starting in each of its blocks.
All inputs are finite; a program needn't handle non-finite values.
Results may differ from a plain program's by a relative error of at most 0.022.
Values may be sent and summed in bfloat16 or wider, within the bound.
A program may use at most 128 MiB of HBM per device.

v0:
```python
import math

import jax
import jax.numpy as jnp
from jax import lax
from jax.sharding import PartitionSpec as P

HEAD_DIM = 64
WIN = 128
QUERY_ROWS = 512


EPSILON = 1e-05
THETA_BASE = 10000.0


def normalize(block_in):
    row_mean = jnp.mean(block_in, axis=-1, keepdims=True)
    centred = block_in - row_mean
    variance = jnp.mean(centred * centred, axis=-1, keepdims=True)
    factor = lax.rsqrt(variance + EPSILON)
    return (centred * factor, factor)


def norm_back(grad_in, normed, factor, gain):
    scaled = grad_in * gain
    centred_grad = (
        scaled
        - jnp.mean(scaled, axis=-1, keepdims=True)
        - normed * jnp.mean(scaled * normed, axis=-1, keepdims=True)
    )
    return (factor * centred_grad, jnp.sum(grad_in * normed, axis=0))


def positions(sequence):
    length = sequence.shape[0]
    row_index = jnp.arange(length, dtype=jnp.int32)
    before = jnp.concatenate([jnp.full((1,), -7, jnp.int32), sequence[:-1]])
    run_start = lax.cummax(jnp.where(sequence != before, row_index, 0), axis=0)
    return row_index - run_start


def rotation(place, width):
    half_width = width // 2
    frequency = jnp.exp(
        jnp.arange(half_width, dtype=jnp.float32) * (-2.0 * math.log(THETA_BASE) / width)
    )
    angles = place.astype(jnp.float32)[:, None] * frequency[None, :]
    return (jnp.cos(angles), jnp.sin(angles))


def rotate(tensor, cosine, sine_table):
    half_width = tensor.shape[-1] // 2
    first_half = tensor[..., :half_width]
    second_half = tensor[..., half_width:]
    cos_rows = cosine[:, None, :]
    sin_rows = sine_table[:, None, :]
    return jnp.concatenate(
        [
            first_half * cos_rows - second_half * sin_rows,
            second_half * cos_rows + first_half * sin_rows,
        ],
        axis=-1,
    )


def rotate_back(tensor, cosine, sine_table):
    half_width = tensor.shape[-1] // 2
    first_half = tensor[..., :half_width]
    second_half = tensor[..., half_width:]
    cos_rows = cosine[:, None, :]
    sin_rows = sine_table[:, None, :]
    return jnp.concatenate(
        [
            first_half * cos_rows + second_half * sin_rows,
            second_half * cos_rows - first_half * sin_rows,
        ],
        axis=-1,
    )


def allowed_pairs(sequence, padded_sequence, offset, half_window, key_span):
    query_seq = lax.dynamic_slice_in_dim(sequence, offset, QUERY_ROWS, 0)
    key_seq = lax.dynamic_slice_in_dim(padded_sequence, offset, key_span, 0)
    query_place = offset + jnp.arange(QUERY_ROWS, dtype=jnp.int32)
    key_place = offset - half_window + jnp.arange(key_span, dtype=jnp.int32)
    distance = jnp.abs(query_place[:, None] - key_place[None, :])
    same_run = (
        (query_seq[:, None] == key_seq[None, :])
        & (query_seq[:, None] >= 0)
        & (distance <= half_window)
    )
    return same_run | (distance == 0)


def block_scores(queries, padded_keys, sequence, padded_sequence, offset, local_heads, half_window):
    key_span = QUERY_ROWS + 2 * half_window
    head_dim = queries.shape[1] // local_heads
    q_block = lax.dynamic_slice_in_dim(queries, offset, QUERY_ROWS, 0).reshape(
        QUERY_ROWS, local_heads, head_dim
    )
    k_block = lax.dynamic_slice_in_dim(padded_keys, offset, key_span, 0).reshape(
        key_span, local_heads, head_dim
    )
    allowed = allowed_pairs(sequence, padded_sequence, offset, half_window, key_span)
    scores = jnp.einsum("qhd,khd->hqk", q_block, k_block, preferred_element_type=jnp.float32) * (
        1.0 / math.sqrt(head_dim)
    )
    return (jnp.where(allowed[None], scores, -1e30), q_block, k_block)


def attend_forward(queries, key_rows, value_rows, sequence, local_heads, half_window):
    group_rows, width = queries.shape
    head_dim = width // local_heads
    key_span = QUERY_ROWS + 2 * half_window
    padded_keys = jnp.pad(key_rows, ((half_window, half_window), (0, 0)))
    padded_values = jnp.pad(value_rows, ((half_window, half_window), (0, 0)))
    padded_sequence = jnp.pad(sequence, (half_window, half_window), constant_values=-5)

    def one_block(offset):
        scores, _, _ = block_scores(
            queries, padded_keys, sequence, padded_sequence, offset, local_heads, half_window
        )
        v_block = lax.dynamic_slice_in_dim(padded_values, offset, key_span, 0).reshape(
            key_span, local_heads, head_dim
        )
        row_peak = jnp.max(scores, axis=-1, keepdims=True)
        weights = jnp.exp(scores - row_peak)
        denominator = jnp.sum(weights, axis=-1, keepdims=True)
        probabilities = (weights / denominator).astype(jnp.bfloat16)
        block_out = jnp.einsum(
            "hqk,khd->qhd", probabilities, v_block, preferred_element_type=jnp.float32
        )
        return (
            block_out.astype(jnp.bfloat16).reshape(QUERY_ROWS, width),
            (row_peak + jnp.log(denominator))[..., 0],
        )

    offsets = jnp.arange(group_rows // QUERY_ROWS, dtype=jnp.int32) * QUERY_ROWS
    outputs, log_totals = lax.map(one_block, offsets)
    return (outputs.reshape(group_rows, width), log_totals)


def attend_backward(
    queries, key_rows, value_rows, sequence, local_heads, half_window, log_totals, grad_mixed
):
    group_rows, width = queries.shape
    head_dim = width // local_heads
    key_span = QUERY_ROWS + 2 * half_window
    factor = 1.0 / math.sqrt(head_dim)
    padded_keys = jnp.pad(key_rows, ((half_window, half_window), (0, 0)))
    padded_values = jnp.pad(value_rows, ((half_window, half_window), (0, 0)))
    padded_sequence = jnp.pad(sequence, (half_window, half_window), constant_values=-5)

    def one_block(accumulated, inputs):
        key_grad, value_grad = accumulated
        offset, log_block = inputs
        scores, q_block, k_block = block_scores(
            queries, padded_keys, sequence, padded_sequence, offset, local_heads, half_window
        )
        v_block = lax.dynamic_slice_in_dim(padded_values, offset, key_span, 0).reshape(
            key_span, local_heads, head_dim
        )
        g_block = lax.dynamic_slice_in_dim(grad_mixed, offset, QUERY_ROWS, 0).reshape(
            QUERY_ROWS, local_heads, head_dim
        )
        probabilities = jnp.exp(scores - log_block[..., None])
        grad_prob = jnp.einsum("qhd,khd->hqk", g_block, v_block, preferred_element_type=jnp.float32)
        inner_sum = jnp.sum(probabilities * grad_prob, axis=-1, keepdims=True)
        grad_score = (probabilities * (grad_prob - inner_sum)).astype(jnp.bfloat16)
        grad_query = (
            jnp.einsum("hqk,khd->qhd", grad_score, k_block, preferred_element_type=jnp.float32)
            * factor
        )
        grad_key = (
            jnp.einsum("hqk,qhd->khd", grad_score, q_block, preferred_element_type=jnp.float32)
            * factor
        )
        grad_value = jnp.einsum(
            "hqk,qhd->khd",
            probabilities.astype(jnp.bfloat16),
            g_block,
            preferred_element_type=jnp.float32,
        )
        key_grad = lax.dynamic_update_slice_in_dim(
            key_grad,
            lax.dynamic_slice_in_dim(key_grad, offset, key_span, 0)
            + grad_key.reshape(key_span, width),
            offset,
            0,
        )
        value_grad = lax.dynamic_update_slice_in_dim(
            value_grad,
            lax.dynamic_slice_in_dim(value_grad, offset, key_span, 0)
            + grad_value.reshape(key_span, width),
            offset,
            0,
        )
        return ((key_grad, value_grad), grad_query.reshape(QUERY_ROWS, width))

    offsets = jnp.arange(group_rows // QUERY_ROWS, dtype=jnp.int32) * QUERY_ROWS
    blank = jnp.zeros((group_rows + 2 * half_window, width), jnp.float32)
    (key_grad, value_grad), query_grad = lax.scan(one_block, (blank, blank), (offsets, log_totals))
    return (
        query_grad.reshape(group_rows, width),
        key_grad[half_window : half_window + group_rows],
        value_grad[half_window : half_window + group_rows],
    )


def body(
    layer_input,
    row_seq,
    qkv_weight,
    out_weight,
    in_weight,
    down_weight,
    attn_gain,
    mlp_gain,
    cotangent,
):
    half_window = WIN // 2
    head_dim = HEAD_DIM
    shards = (qkv_weight, out_weight, in_weight, down_weight, attn_gain, mlp_gain)
    w_qkv, w_out, w_in, w_down, gain_one, gain_two = (
        lax.all_gather(shards[0], "dp", axis=0, tiled=True),
        lax.all_gather(shards[1], "dp", axis=1, tiled=True),
        lax.all_gather(shards[2], "dp", axis=0, tiled=True),
        lax.all_gather(shards[3], "dp", axis=1, tiled=True),
        lax.all_gather(shards[4], "dp", axis=0, tiled=True),
        lax.all_gather(shards[5], "dp", axis=0, tiled=True),
    )
    gain_one = gain_one.astype(jnp.float32)
    gain_two = gain_two.astype(jnp.float32)
    block_in = layer_input.astype(jnp.float32)
    normed_one, factor_one = normalize(block_in)
    h_one = (normed_one * gain_one).astype(jnp.bfloat16)
    h_all, seq_all = (
        lax.all_gather(h_one, "mp", axis=0, tiled=True),
        lax.all_gather(row_seq, "mp", axis=0, tiled=True),
    )
    group_rows = h_all.shape[0]
    width = w_qkv.shape[2]
    local_heads = width // head_dim
    qkv = jnp.einsum("rd,dcf->rcf", h_all, w_qkv, preferred_element_type=jnp.float32)
    cosine, sine_table = rotation(positions(seq_all), head_dim)
    queries = (
        rotate(qkv[:, 0].reshape(group_rows, local_heads, head_dim), cosine, sine_table)
        .reshape(group_rows, width)
        .astype(jnp.bfloat16)
    )
    key_rows = (
        rotate(qkv[:, 1].reshape(group_rows, local_heads, head_dim), cosine, sine_table)
        .reshape(group_rows, width)
        .astype(jnp.bfloat16)
    )
    value_rows = qkv[:, 2].astype(jnp.bfloat16)
    mixed_heads, log_totals = attend_forward(
        queries, key_rows, value_rows, seq_all, local_heads, half_window
    )
    middle = block_in + lax.psum_scatter(
        jnp.dot(mixed_heads, w_out, preferred_element_type=jnp.float32).astype(jnp.bfloat16),
        "mp",
        scatter_dimension=0,
        tiled=True,
    ).astype(jnp.float32)
    normed_two, factor_two = normalize(middle)
    h_two = (normed_two * gain_two).astype(jnp.bfloat16)
    h2_all = lax.all_gather(h_two, "mp", axis=0, tiled=True)
    gate_up = jnp.einsum("rd,dcf->rcf", h2_all, w_in, preferred_element_type=jnp.float32)
    gate_vals = gate_up[:, 0]
    up_values = gate_up[:, 1]
    hidden = (jax.nn.gelu(gate_vals, approximate=False) * up_values).astype(jnp.bfloat16)
    final_rows = middle + lax.psum_scatter(
        jnp.dot(hidden, w_down, preferred_element_type=jnp.float32).astype(jnp.bfloat16),
        "mp",
        scatter_dimension=0,
        tiled=True,
    ).astype(jnp.float32)
    activations = final_rows.astype(jnp.bfloat16)
    w_qkv, w_out, w_in, w_down, gain_one, gain_two = (
        lax.all_gather(shards[0], "dp", axis=0, tiled=True),
        lax.all_gather(shards[1], "dp", axis=1, tiled=True),
        lax.all_gather(shards[2], "dp", axis=0, tiled=True),
        lax.all_gather(shards[3], "dp", axis=1, tiled=True),
        lax.all_gather(shards[4], "dp", axis=0, tiled=True),
        lax.all_gather(shards[5], "dp", axis=0, tiled=True),
    )
    gain_one = gain_one.astype(jnp.float32)
    gain_two = gain_two.astype(jnp.float32)
    live_rows = (row_seq >= 0).astype(jnp.float32)[:, None]
    grad_final = cotangent.astype(jnp.float32) * live_rows
    grad_all = lax.all_gather(grad_final.astype(jnp.bfloat16), "mp", axis=0, tiled=True)
    down_grad = lax.dot_general(
        hidden, grad_all, (((0,), (0,)), ((), ())), preferred_element_type=jnp.float32
    )
    grad_hidden = lax.dot_general(
        grad_all, w_down, (((1,), (1,)), ((), ())), preferred_element_type=jnp.float32
    )

    def product(gate_in, up_in):
        return jax.nn.gelu(gate_in, approximate=False) * up_in

    _, pullback = jax.vjp(product, gate_vals, up_values)
    grad_gate, grad_up = pullback(grad_hidden)
    grad_both = jnp.stack([grad_gate, grad_up], axis=1).astype(jnp.bfloat16)
    in_grad = jnp.einsum("rd,rcf->dcf", h2_all, grad_both, preferred_element_type=jnp.float32)
    grad_h_two = lax.psum_scatter(
        jnp.einsum("rcf,dcf->rd", grad_both, w_in, preferred_element_type=jnp.float32).astype(
            jnp.bfloat16
        ),
        "mp",
        scatter_dimension=0,
        tiled=True,
    ).astype(jnp.float32)
    grad_norm_two, gain_two_grad = norm_back(grad_h_two, normed_two, factor_two, gain_two)
    grad_middle = grad_final + grad_norm_two
    grad_mid_all = lax.all_gather(grad_middle.astype(jnp.bfloat16), "mp", axis=0, tiled=True)
    out_grad = lax.dot_general(
        mixed_heads, grad_mid_all, (((0,), (0,)), ((), ())), preferred_element_type=jnp.float32
    )
    grad_mixed = lax.dot_general(
        grad_mid_all, w_out, (((1,), (1,)), ((), ())), preferred_element_type=jnp.float32
    ).astype(jnp.bfloat16)
    grad_query, grad_key, grad_value = attend_backward(
        queries, key_rows, value_rows, seq_all, local_heads, half_window, log_totals, grad_mixed
    )
    grad_query = rotate_back(
        grad_query.reshape(group_rows, local_heads, head_dim), cosine, sine_table
    ).reshape(group_rows, width)
    grad_key = rotate_back(
        grad_key.reshape(group_rows, local_heads, head_dim), cosine, sine_table
    ).reshape(group_rows, width)
    grad_qkv = jnp.stack([grad_query, grad_key, grad_value], axis=1).astype(jnp.bfloat16)
    qkv_grad = jnp.einsum("rd,rcf->dcf", h_all, grad_qkv, preferred_element_type=jnp.float32)
    grad_h_one = lax.psum_scatter(
        jnp.einsum("rcf,dcf->rd", grad_qkv, w_qkv, preferred_element_type=jnp.float32).astype(
            jnp.bfloat16
        ),
        "mp",
        scatter_dimension=0,
        tiled=True,
    ).astype(jnp.float32)
    grad_norm_one, gain_one_grad = norm_back(grad_h_one, normed_one, factor_one, gain_one)
    input_grad = (grad_middle + grad_norm_one).astype(jnp.bfloat16)
    qkv_share, out_share, in_share, down_share, gain_one_share, gain_two_share = (
        lax.psum_scatter(qkv_grad, "dp", scatter_dimension=0, tiled=True),
        lax.psum_scatter(out_grad, "dp", scatter_dimension=1, tiled=True),
        lax.psum_scatter(in_grad, "dp", scatter_dimension=0, tiled=True),
        lax.psum_scatter(down_grad, "dp", scatter_dimension=1, tiled=True),
        lax.psum_scatter(gain_one_grad, "dp", scatter_dimension=0, tiled=True),
        lax.psum_scatter(gain_two_grad, "dp", scatter_dimension=0, tiled=True),
    )
    gain_one_total, gain_two_total = lax.psum((gain_one_share, gain_two_share), "mp")
    return (
        activations,
        input_grad,
        gain_one_total,
        gain_two_total,
        qkv_share,
        out_share,
        in_share,
        down_share,
    )


def solution(mesh):
    in_specs = (
        P(("dp", "mp"), None),
        P(("dp", "mp")),
        P("dp", None, "mp"),
        P("mp", "dp"),
        P("dp", None, "mp"),
        P("mp", "dp"),
        P("dp"),
        P("dp"),
        P(("dp", "mp"), None),
    )
    out_specs = (
        P(("dp", "mp"), None),
        P(("dp", "mp"), None),
        P("dp"),
        P("dp"),
        P("dp", None, "mp"),
        P("mp", "dp"),
        P("dp", None, "mp"),
        P("mp", "dp"),
    )
    return jax.shard_map(body, mesh=mesh, in_specs=in_specs, out_specs=out_specs, check_vma=False)
```

profile of v0, /device:TPU:0, one launch (start us, length us, event | category | flops | bytes accessed | tf_op | source)
XLA Modules:
  0.0 1040.3 jit_solution(17701184751607131137)
XLA Ops:
  9.1 22.3 %all-gather = bf16[8,1,128]{2,1,0:T(2,128)(2,1)S(1)} all-gather(bf16[1,1,128]{2,1,0:T(2,128)(2,1)} %bitcast.270), channel_id=1, replica_groups=mesh['dp'=8,'mp'=4] {'dp'}, dimensions={0}, use_global_device_ids=true | all-gather | bytes 2304 | tf_op jit(solution)/shard_map/all_gather | solution.py:230
  43.2 29.2 %all_gather.43 = bf16[256,1024]{1,0:T(8,128)(2,1)S(1)} all-gather(bf16[256,128]{1,0:T(8,128)(2,1)S(1)} %copy-done.26), channel_id=1, replica_groups=mesh['dp'=8,'mp'=4] {'dp'}, dimensions={1}, use_global_device_ids=true | all-gather | bytes 589824 | tf_op jit(solution)/shard_map/all_gather | solution.py:227
  73.1 21.1 %all-gather.11.cloned.1.call-done = bf16[1536,1024]{1,0:T(8,128)(2,1)} async-done(((bf16[384,1024]{1,0:T(8,128)(2,1)}), bf16[1536,1024]{1,0:T(8,128)(2,1)}) %all-gather.11.cloned.1.call-update) | async-done | bytes 3145744 | tf_op jit(solution)/shard_map/all_gather | solution.py:239
  103.6 40.8 %while.30 = (s32[]{:T(128)}, bf16[3,512,256]{2,1,0:T(8,128)(2,1)S(1)}, f32[3,4,512]{2,1,0:T(4,128)S(1)}, s32[3]{0:T(128)S(1)}, bf16[1664,256]{0,1:T(8,128)(2,1)}...) while((s32[]{:T(128)}, ...), condition=%wide.region_7.8_spmd, body=%wide.region_4.7_spmd.sunk | while | flops 354025088 | bytes 21192440 | solution.py:140
  150.8 20.4 %all-gather.2 = bf16[8,1,128]{2,1,0:T(2,128)(2,1)S(1)} all-gather(bf16[1,1,128]{2,1,0:T(2,128)(2,1)S(1)} %bitcast.271), channel_id=1, replica_groups=mesh['dp'=8,'mp'=4] {'dp'}, dimensions={0}, use_global_device_ids=true | all-gather | bytes 2304 | tf_op jit(solution)/shard_map/all_gather | solution.py:231
  171.2 14.9 %reduce-scatter.9.cloned.1.call-done = bf16[384,1024]{1,0:T(8,128)(2,1)} async-done(((bf16[1536,1024]{1,0:T(8,128)(2,1)}), bf16[384,1024]{1,0:T(8,128)(2,1)}) %reduce-scatter.9.cloned.1.call-update) | async-done | bytes 786448 | tf_op jit(solution)/shard_map/reduce_scatter | solution.py:261
  190.4 40.4 %all-gather.19.cloned.1.call-done = bf16[656,1024]{1,0:T(8,128)(2,1)} async-done(((bf16[656,128]{1,0:T(8,128)(2,1)}), bf16[656,1024]{1,0:T(8,128)(2,1)}) %all-gather.19.cloned.1.call-update) | async-done | bytes 1343504 | tf_op jit(solution)/shard_map/all_gather | solution.py:229
  230.8 29.3 %all-gather.21.cloned.1.call-done = bf16[1536,1024]{1,0:T(8,128)(2,1)} async-done(((bf16[384,1024]{1,0:T(8,128)(2,1)}), bf16[1536,1024]{1,0:T(8,128)(2,1)}) %all-gather.21.cloned.1.call-update) | async-done | bytes 3145744 | tf_op jit(solution)/shard_map/all_gather | solution.py:293
  260.1 6.4 fusion.87
  266.5 53.3 %all-gather.17.cloned.1.call-done = bf16[1024,2,656]{0,2,1:T(8,128)(2,1)} async-done(((bf16[128,2,656]{0,2,1:T(8,128)(2,1)}), bf16[1024,2,656]{0,2,1:T(8,128)(2,1)}) %all-gather.17.cloned.1.call-update) | async-done | bytes 2686992 | tf_op jit(solution)/shard_map/all_gather | solution.py:228
  319.8 29.0 %all-gather.15.cloned.1.call-done = bf16[1536,1024]{1,0:T(8,128)(2,1)} async-done(((bf16[384,1024]{1,0:T(8,128)(2,1)}), bf16[1536,1024]{1,0:T(8,128)(2,1)}) %all-gather.15.cloned.1.call-update) | async-done | bytes 3145744 | tf_op jit(solution)/shard_map/all_gather | solution.py:269
  348.8 7.2 fusion.42
  356.1 10.7 %fusion.49 = (bf16[1536,1,656]{0,2,1:T(8,128)(2,1)}, f32[1536,656]{0,1:T(8,128)}) fusion(f32[1536,656]{0,1:T(8,128)S(1)} %copy-done.9, f32[1536,2,656]{0,2,1:T(8,128)S(1)} %fusion.42), kind=kLoop, calls=%fused_computation.99 | loop fusion | flops 73555968 | bytes 18137088 | tf_op jit(solution)/shard_map/stack | solution.py:306
  366.8 7.4 fusion.48
  374.1 8.8 bitcast_convert_fusion.1
  383.0 12.2 %reduce-scatter.11.cloned.1.call-start = ((), (), s32[]{:S(2)}) async-start(), calls=%async_computation.14 | async-start | bytes 3932160 | tf_op jit(solution)/shard_map/reduce_scatter | solution.py:274
  401.6 19.5 %reduce-scatter.13.cloned.1.call-done = bf16[384,1024]{1,0:T(8,128)(2,1)} async-done(((bf16[1536,1024]{1,0:T(8,128)(2,1)}), bf16[384,1024]{1,0:T(8,128)(2,1)}) %reduce-scatter.13.cloned.1.call-update) | async-done | bytes 786448 | tf_op jit(solution)/shard_map/reduce_scatter | solution.py:308
  423.1 38.6 %reduce-scatter.11.cloned.1.call-done = bf16[384,1024]{1,0:T(8,128)(2,1)} async-done(((bf16[1536,1024]{1,0:T(8,128)(2,1)}), bf16[384,1024]{1,0:T(8,128)(2,1)}) %reduce-scatter.11.cloned.1.call-update) | async-done | bytes 786448 | tf_op jit(solution)/shard_map/reduce_scatter | solution.py:274
  465.7 28.6 %all-gather.23.cloned.1.call-done = bf16[1536,1024]{1,0:T(8,128)(2,1)} async-done(((bf16[384,1024]{1,0:T(8,128)(2,1)}), bf16[1536,1024]{1,0:T(8,128)(2,1)}) %all-gather.23.cloned.1.call-update) | async-done | bytes 3145744 | tf_op jit(solution)/shard_map/all_gather | solution.py:318
  500.7 146.9 %while.31 = (s32[]{:T(128)}, f32[1664,256]{0,1:T(8,128)}, f32[1664,256]{1,0:T(8,128)}, f32[3,512,256]{1,0,2:T(4,128)}, s32[3]{0:T(128)S(1)}, /*index=5*/bf16[153...) while((s32[]{:T(128)}, f32[1664,256]{0,1:T(8,128)}, ...), condition=%wide.region_17.18_spmd, body=%wide.region_15.17_spmd.sunk | while | flops 861765248 | bytes 84164640 | solution.py:203
  522.8 11.1 %dynamic_update_slice.44 = f32[3,512,256]{1,0,2:T(4,128)} dynamic-update-slice(f32[3,512,256]{1,0,2:T(4,128)} %get-tuple-element.617, f32[1,512,256]{1,0,2:T(1,128)} %copy.74, s32[]{:T(128)} %get-tuple-element.614, s32[]{:T(128)} %constant.172.clone.1..sunk.1, s32[]{:T(128)} %constant.172.clone.1..sunk.1) | dynamic-update-slice | bytes 1048580 | tf_op jit(solution)/shard_map/while/body/jit(dynamic_update_index_in_dim)/dynamic_update_slice | solution.py:203
  572.1 11.1 %dynamic_update_slice.44 = f32[3,512,256]{1,0,2:T(4,128)} dynamic-update-slice(f32[3,512,256]{1,0,2:T(4,128)} %get-tuple-element.617, f32[1,512,256]{1,0,2:T(1,128)} %copy.74, s32[]{:T(128)} %get-tuple-element.614, s32[]{:T(128)} %constant.172.clone.1..sunk.1, s32[]{:T(128)} %constant.172.clone.1..sunk.1) | dynamic-update-slice | bytes 1048580 | tf_op jit(solution)/shard_map/while/body/jit(dynamic_update_index_in_dim)/dynamic_update_slice | solution.py:203
  621.3 11.1 %dynamic_update_slice.44 = f32[3,512,256]{1,0,2:T(4,128)} dynamic-update-slice(f32[3,512,256]{1,0,2:T(4,128)} %get-tuple-element.617, f32[1,512,256]{1,0,2:T(1,128)} %copy.74, s32[]{:T(128)} %get-tuple-element.614, s32[]{:T(128)} %constant.172.clone.1..sunk.1, s32[]{:T(128)} %constant.172.clone.1..sunk.1) | dynamic-update-slice | bytes 1048580 | tf_op jit(solution)/shard_map/while/body/jit(dynamic_update_index_in_dim)/dynamic_update_slice | solution.py:203
  670.6 10.0 fusion.40
  685.8 6.4 fusion.44
  694.1 7.8 reduce-scatter.15.cloned.1.call-done
  703.8 21.9 %all-reduce.5 = (f32[1024]{0:T(1024)S(1)}, f32[1024]{0:T(1024)S(1)}) all-reduce(f32[1024]{0:T(1024)S(1)} %get-tuple-element.316, f32[1024]{0:T(1024)S(1)} %get-tuple-element.314), channel_id=6, replica_groups=mesh['dp'=8,'mp'=4] {'dp'}, use_global_device_ids=true, to_apply=%region_22.23.clone | all-reduce | flops 2048 | bytes 16384
  725.8 6.5 all-reduce.6
  735.0 44.1 %reduce-scatter.23.cloned.1.call-done = f32[656,128]{1,0:T(8,128)} async-done(((f32[656,1024]{1,0:T(8,128)}), f32[656,128]{1,0:T(8,128)}) %reduce-scatter.23.cloned.1.call-update) | async-done | bytes 335888 | tf_op jit(solution)/shard_map/reduce_scatter | solution.py:350
  779.1 108.2 %reduce-scatter.21.cloned.1.call-done = f32[128,2,656]{0,2,1:T(8,128)} async-done(((f32[1024,2,656]{0,2,1:T(8,128)}), f32[128,2,656]{0,2,1:T(8,128)}) %reduce-scatter.21.cloned.1.call-update) | async-done | bytes 671760 | tf_op jit(solution)/shard_map/reduce_scatter | solution.py:349
  887.3 67.5 %reduce-scatter.19.cloned.1.call-done = f32[256,128]{1,0:T(8,128)} async-done(((f32[256,1024]{1,0:T(8,128)}), f32[256,128]{1,0:T(8,128)}) %reduce-scatter.19.cloned.1.call-update) | async-done | bytes 131088 | tf_op jit(solution)/shard_map/reduce_scatter | solution.py:348
  954.8 78.6 %reduce-scatter.17.cloned.1.call-done = f32[128,3,256]{2,0,1:T(8,128)} async-done(((f32[1024,3,256]{2,0,1:T(8,128)}), f32[128,3,256]{2,0,1:T(8,128)}) %reduce-scatter.17.cloned.1.call-update) | async-done | bytes 393232 | tf_op jit(solution)/shard_map/reduce_scatter | solution.py:347
  (324 shorter events, 217.1 us)
Async XLA Ops:
  7.2 30.0 %copy-start.31 = (s32[384]{0:T(512)S(1)}, s32[384]{0:T(512)}, u32[]{:S(2)}) copy-start(s32[384]{0:T(512)} %param.14) | copy-start | bytes 4612
  7.2 36.0 %copy-start.26 = (bf16[256,128]{1,0:T(8,128)(2,1)S(1)}, bf16[256,128]{1,0:T(8,128)(2,1)}, u32[]{:S(2)}) copy-start(bf16[256,128]{1,0:T(8,128)(2,1)} %param.16) | copy-start | bytes 196612
  7.2 65.9 %all-gather.13.cloned.1.call-start = ((), (), s32[]{:S(2)}) async-start(), calls=%async_computation.9 | async-start | bytes 1769472 | tf_op jit(solution)/shard_map/all_gather | solution.py:226
  9.0 85.2 %all-gather.11.cloned.1.call-start = ((), (), s32[]{:S(2)}) async-start(), calls=%async_computation.8 | async-start | bytes 3932160 | tf_op jit(solution)/shard_map/all_gather | solution.py:239
  37.1 149.0 %reduce-scatter.9.cloned.1.call-start = ((), (), s32[]{:S(2)}) async-start(), calls=%async_computation.10 | async-start | bytes 3932160 | tf_op jit(solution)/shard_map/reduce_scatter | solution.py:261
  73.1 26.4 %copy-start.15 = (f32[1536,32]{0,1:T(8,128)}, f32[1536,32]{0,1:T(8,128)S(1)}, u32[]{:S(2)}) copy-start(f32[1536,32]{0,1:T(8,128)S(1)} %get-tuple-element.399) | copy-start | bytes 589828
  73.1 26.4 %copy-start.17 = (f32[1536,32]{0,1:T(8,128)}, f32[1536,32]{0,1:T(8,128)S(1)}, u32[]{:S(2)}) copy-start(f32[1536,32]{0,1:T(8,128)S(1)} %get-tuple-element.400) | copy-start | bytes 589828
  147.9 38.1 %copy-start = (bf16[384,1024]{1,0:T(8,128)(2,1)S(1)}, bf16[384,1024]{1,0:T(8,128)(2,1)}, u32[]{:S(2)}) copy-start(bf16[384,1024]{1,0:T(8,128)(2,1)} %param.13) | copy-start | bytes 2359300
  148.0 82.9 %all-gather.19.cloned.1.call-start = ((), (), s32[]{:S(2)}) async-start(), calls=%async_computation.13 | async-start | bytes 1511424 | tf_op jit(solution)/shard_map/all_gather | solution.py:229
  148.5 111.5 %all-gather.21.cloned.1.call-start = ((), (), s32[]{:S(2)}) async-start(), calls=%async_computation.15 | async-start | bytes 3932160 | tf_op jit(solution)/shard_map/all_gather | solution.py:293
  150.2 169.7 %all-gather.17.cloned.1.call-start = ((), (), s32[]{:S(2)}) async-start(), calls=%async_computation.12 | async-start | bytes 3022848 | tf_op jit(solution)/shard_map/all_gather | solution.py:228
  150.7 198.1 %all-gather.15.cloned.1.call-start = ((), (), s32[]{:S(2)}) async-start(), calls=%async_computation.11 | async-start | bytes 3932160 | tf_op jit(solution)/shard_map/all_gather | solution.py:269
  190.4 230.7 %reduce-scatter.13.cloned.1.call-start = ((), (), s32[]{:S(2)}) async-start(), calls=%async_computation.16 | async-start | bytes 3932160 | tf_op jit(solution)/shard_map/reduce_scatter | solution.py:308
  348.8 7.2 copy-start.9
  383.0 78.6 %reduce-scatter.11.cloned.1.call-start = ((), (), s32[]{:S(2)}) async-start(), calls=%async_computation.14 | async-start | bytes 3932160 | tf_op jit(solution)/shard_map/reduce_scatter | solution.py:274
  401.5 92.8 %all-gather.23.cloned.1.call-start = ((), (), s32[]{:S(2)}) async-start(), calls=%async_computation.17 | async-start | bytes 3932160 | tf_op jit(solution)/shard_map/all_gather | solution.py:318
  465.6 236.3 %reduce-scatter.15.cloned.1.call-start = ((), (), s32[]{:S(2)}) async-start(), calls=%async_computation.18 | async-start | bytes 3932160 | tf_op jit(solution)/shard_map/reduce_scatter | solution.py:336
  535.5 6.0 copy-start.2
  535.5 6.0 copy-start.7
  647.7 6.1 copy-start.16
  647.7 6.1 copy-start.18
  656.0 7.8 copy-start.19
  656.3 7.4 copy-start.21
  663.8 6.7 copy-start.14
  663.8 115.2 %reduce-scatter.23.cloned.1.call-start = ((), (), s32[]{:S(2)}) async-start(), calls=%async_computation.22 | async-start | bytes 3022848 | tf_op jit(solution)/shard_map/reduce_scatter | solution.py:350
  670.5 216.8 %reduce-scatter.21.cloned.1.call-start = ((), (), s32[]{:S(2)}) async-start(), calls=%async_computation.21 | async-start | bytes 6045696 | tf_op jit(solution)/shard_map/reduce_scatter | solution.py:349
  680.6 274.3 %reduce-scatter.19.cloned.1.call-start = ((), (), s32[]{:S(2)}) async-start(), calls=%async_computation.20 | async-start | bytes 1179648 | tf_op jit(solution)/shard_map/reduce_scatter | solution.py:348
  685.7 347.7 %reduce-scatter.17.cloned.1.call-start = ((), (), s32[]{:S(2)}) async-start(), calls=%async_computation.19 | async-start | bytes 3538944 | tf_op jit(solution)/shard_map/reduce_scatter | solution.py:347
  692.2 9.7 copy-start.25
  692.2 9.7 copy-start.28
  692.2 9.7 copy-start.30
  692.2 40.2 %copy-start.10 = (f32[384,1024]{1,0:T(8,128)S(1)}, f32[384,1024]{1,0:T(8,128)}, u32[]{:S(2)}) copy-start(f32[384,1024]{1,0:T(8,128)} %get-tuple-element.371) | copy-start | bytes 4718596
  (37 other events, 141.0 us)
Sparse Core Ops, SparseCore 0:
  10.6 51.5 all-gather.12
  64.4 29.7 all-gather.10
  148.1 37.9 reduce-scatter.8
  188.2 42.5 all-gather.18
  232.9 27.1 all-gather.20
  262.2 57.6 all-gather.16
  322.1 26.7 all-gather.14
  383.1 37.9 reduce-scatter.12
  423.6 37.9 reduce-scatter.10
  465.7 28.5 all-gather.22
  663.9 37.9 reduce-scatter.14
  705.8 73.2 reduce-scatter.22
  783.7 103.5 reduce-scatter.20
  891.1 63.6 reduce-scatter.18
  959.3 74.0 reduce-scatter.16
where the time goes:
time: 1050 us; the launch traced here: 1040 us
  waiting for transfers between devices  582 us (55%)
  matrix products  124 us (12%)
  local copies, waits for them, and re-layouts  107 us (10%)
  blocking collectives  105 us (10%)
  other arithmetic  68.8 us (7%)
  loops' own time  24.3 us (2%)
  between operations  15.4 us (1%)
  starting transfers between devices  13.2 us (1%)
    reduce_scatter x1, waiting for transfers between devices, body(): lax.psum_scatter(in_grad, 'dp', scatter_dimension=0, tiled=True)  108 us
    reduce_scatter x1, waiting for transfers between devices, body(): lax.psum_scatter(qkv_grad, 'dp', scatter_dimension=0, tiled=True)  78.6 us
    reduce_scatter x1, waiting for transfers between devices, body(): lax.psum_scatter(out_grad, 'dp', scatter_dimension=1, tiled=True)  67.5 us
    all_gather x1, waiting for transfers between devices, body(): lax.all_gather(shards[2], 'dp', axis=0, tiled=True)  53.3 us
    reduce_scatter x1, waiting for transfers between devices, body(): lax.psum_scatter(down_grad, 'dp', scatter_dimension=1, tiled=True)  44.1 us
    all_gather x1, waiting for transfers between devices, body(): lax.all_gather(shards[3], 'dp', axis=1, tiled=True)  40.4 us
    reduce_scatter x1, waiting for transfers between devices, body(): lax.psum_scatter(jnp.dot(hidden, w_down, preferred_element_type=jnp.float...  38.6 us
    dynamic_update_slice x6, local copies, waits for them, and re-layouts, attend_backward(): lax.scan(one_block, (blank, blank), (offsets, log_totals))  37.2 us
  transfers between devices with their start and end apart: 15, of which 14 were waited for; matrix products, arithmetic and copies ran while one was open for 6% of the time, Pallas kernels for 0%

commit v1 on v0

v1 whole, which is shorter than its diff:
```python
import math

import jax
import jax.numpy as jnp
from jax import lax
from jax.experimental import pallas as pl
from jax.experimental.pallas import tpu as pltpu
from jax.sharding import PartitionSpec as P

HEAD_DIM = 64
WIN = 128
EPSILON = 1e-05
THETA_BASE = 10000.0
BF16 = jnp.bfloat16
F32 = jnp.float32


def normalize(block_in):
    row_mean = jnp.mean(block_in, axis=-1, keepdims=True)
    centred = block_in - row_mean
    variance = jnp.mean(centred * centred, axis=-1, keepdims=True)
    factor = lax.rsqrt(variance + EPSILON)
    return (centred * factor, factor)


def norm_back(grad_in, normed, factor, gain):
    scaled = grad_in * gain
    centred_grad = (
        scaled
        - jnp.mean(scaled, axis=-1, keepdims=True)
        - normed * jnp.mean(scaled * normed, axis=-1, keepdims=True)
    )
    return (factor * centred_grad, jnp.sum(grad_in * normed, axis=0))


def positions(sequence):
    length = sequence.shape[0]
    row_index = jnp.arange(length, dtype=jnp.int32)
    before = jnp.concatenate([jnp.full((1,), -7, jnp.int32), sequence[:-1]])
    run_start = lax.cummax(jnp.where(sequence != before, row_index, 0), axis=0)
    return row_index - run_start


def rotation_tables(place):
    half = HEAD_DIM // 2
    frequency = jnp.exp(
        jnp.arange(half, dtype=F32) * (-2.0 * math.log(THETA_BASE) / HEAD_DIM)
    )
    angles = place.astype(F32)[:, None] * frequency[None, :]
    cosine, sine = (jnp.cos(angles), jnp.sin(angles))
    return (
        jnp.concatenate([cosine] * 4, axis=1),
        jnp.concatenate([-sine, sine, -sine, sine], axis=1),
    )


def turn(tensor, cosine, signed_sine):
    lane = lax.broadcasted_iota(jnp.int32, cosine.shape, 1)
    first = (lane % HEAD_DIM) < HEAD_DIM // 2
    parts = []
    for start in range(0, tensor.shape[1], 128):
        piece = tensor[:, start : start + 128]
        other = jnp.where(first, pltpu.roll(piece, 96, 1), pltpu.roll(piece, 32, 1))
        parts.append(piece * cosine + other * signed_sine)
    return jnp.concatenate(parts, axis=1)


def head_masks(heads, width):
    lane = lax.broadcasted_iota(jnp.int32, (WIN, width), 1)
    return [(lane // HEAD_DIM == head).astype(F32) for head in range(heads)]


def allowed_pairs(seq_col, seq_row):
    query = lax.broadcasted_iota(jnp.int32, (WIN, 2 * WIN), 0) + WIN // 2
    key = lax.broadcasted_iota(jnp.int32, (WIN, 2 * WIN), 1)
    distance = jnp.abs(query - key)
    same_run = (seq_col == seq_row) & (seq_col >= 0) & (distance <= WIN // 2)
    return same_run | (distance == 0)


def place_of(block, me, per_quarter):
    quarter = lax.div(block, per_quarter)
    start = pl.multiple_of(lax.rem(block, per_quarter) * WIN, WIN)
    return (jnp.bitwise_xor(quarter, me), pl.ds(start, WIN))


def probabilities_of(queries, keys, allowed, masks):
    heads = len(masks)
    stacked = jnp.concatenate([queries * mask.astype(BF16) for mask in masks], axis=0)
    scores = lax.dot_general(
        stacked, keys, (((1,), (1,)), ((), ())), preferred_element_type=F32
    ) * (1.0 / math.sqrt(HEAD_DIM))
    scores = scores.reshape(heads, WIN, 2 * WIN)
    scores = jnp.where(allowed[None], scores, -1e30)
    weights = jnp.exp(scores - jnp.max(scores, axis=-1, keepdims=True))
    total = jnp.sum(weights, axis=-1, keepdims=True)
    return (stacked, weights * (1.0 / total))


def forward_kernel(me_ref, qkv_ref, cos_ref, sin_ref, col_ref, row_ref, o_ref, q_ref, k_ref, v_ref):
    me = me_ref[0]
    rows, width = q_ref.shape
    blocks = rows // WIN
    per_quarter = qkv_ref.shape[1] // WIN
    half = WIN // 2
    for ref in (k_ref, v_ref):
        ref[0:half, :] = jnp.zeros((half, width), BF16)
        ref[rows + half : rows + 2 * half, :] = jnp.zeros((half, width), BF16)

    def turn_block(block, carry):
        quarter, inner = place_of(block, me, per_quarter)
        start = pl.multiple_of(block * WIN, WIN)
        here = pl.ds(start, WIN)
        later = pl.ds(pl.multiple_of(start + half, half), WIN)
        cosine, sine = (cos_ref[here, :], sin_ref[here, :])
        q_ref[here, :] = turn(qkv_ref[quarter, inner, 0:width], cosine, sine).astype(BF16)
        k_ref[later, :] = turn(qkv_ref[quarter, inner, width : 2 * width], cosine, sine).astype(BF16)
        v_ref[later, :] = qkv_ref[quarter, inner, 2 * width : 3 * width].astype(BF16)
        return carry

    lax.fori_loop(0, blocks, turn_block, 0)
    masks = head_masks(width // HEAD_DIM, width)

    def attend_block(block, carry):
        quarter, inner = place_of(block, me, per_quarter)
        start = pl.multiple_of(block * WIN, WIN)
        span = pl.ds(start, 2 * WIN)
        allowed = allowed_pairs(col_ref[pl.ds(start, WIN), :], row_ref[block])
        _, prob = probabilities_of(q_ref[pl.ds(start, WIN), :], k_ref[span, :], allowed, masks)
        prob = prob.astype(BF16).reshape(-1, 2 * WIN)
        mixed = jnp.dot(prob, v_ref[span, :], preferred_element_type=F32)
        mixed = mixed.reshape(len(masks), WIN, width)
        o_ref[quarter, inner, :] = sum(
            mixed[head] * mask for head, mask in enumerate(masks)
        ).astype(BF16)
        return carry

    lax.fori_loop(0, blocks, attend_block, 0)


def backward_kernel(
    me_ref, q_ref, k_ref, v_ref, g_ref, cos_ref, sin_ref, col_ref, row_ref, d_ref, dk_ref, dv_ref
):
    me = me_ref[0]
    rows, width = q_ref.shape
    blocks = rows // WIN
    per_quarter = g_ref.shape[1] // WIN
    half = WIN // 2
    factor = 1.0 / math.sqrt(HEAD_DIM)
    dk_ref[...] = jnp.zeros(dk_ref.shape, F32)
    dv_ref[...] = jnp.zeros(dv_ref.shape, F32)
    masks = head_masks(width // HEAD_DIM, width)
    over_rows = (((0,), (0,)), ((), ()))

    def attend_block(block, carry):
        quarter, inner = place_of(block, me, per_quarter)
        start = pl.multiple_of(block * WIN, WIN)
        here = pl.ds(start, WIN)
        span = pl.ds(start, 2 * WIN)
        allowed = allowed_pairs(col_ref[here, :], row_ref[block])
        keys = k_ref[span, :]
        queries, prob = probabilities_of(q_ref[here, :], keys, allowed, masks)
        grads = g_ref[quarter, inner, :]
        grads = jnp.concatenate([grads * mask.astype(BF16) for mask in masks], axis=0)
        grad_prob = lax.dot_general(
            grads, v_ref[span, :], (((1,), (1,)), ((), ())), preferred_element_type=F32
        ).reshape(prob.shape)
        inner_sum = jnp.sum(prob * grad_prob, axis=-1, keepdims=True)
        grad_score = (prob * (grad_prob - inner_sum)).astype(BF16).reshape(-1, 2 * WIN)
        prob = prob.astype(BF16).reshape(-1, 2 * WIN)
        dv_ref[span, :] += lax.dot_general(prob, grads, over_rows, preferred_element_type=F32)
        dk_ref[span, :] += lax.dot_general(
            grad_score, queries, over_rows, preferred_element_type=F32
        )
        grad_query = jnp.dot(grad_score, keys, preferred_element_type=F32)
        grad_query = grad_query.reshape(len(masks), WIN, width)
        grad_query = sum(grad_query[head] * mask for head, mask in enumerate(masks)) * factor
        d_ref[quarter, inner, 0:width] = turn(
            grad_query, cos_ref[here, :], -sin_ref[here, :]
        ).astype(BF16)
        return carry

    lax.fori_loop(0, blocks, attend_block, 0)

    def finish_block(block, carry):
        quarter, inner = place_of(block, me, per_quarter)
        start = pl.multiple_of(block * WIN, WIN)
        here = pl.ds(start, WIN)
        later = pl.ds(pl.multiple_of(start + half, half), WIN)
        d_ref[quarter, inner, width : 2 * width] = turn(
            dk_ref[later, :] * factor, cos_ref[here, :], -sin_ref[here, :]
        ).astype(BF16)
        d_ref[quarter, inner, 2 * width : 3 * width] = dv_ref[later, :].astype(BF16)
        return carry

    lax.fori_loop(0, blocks, finish_block, 0)


def vmem_specs(count):
    return [pl.BlockSpec(memory_space=pltpu.SMEM)] + [pl.BlockSpec(memory_space=pltpu.VMEM)] * count


def attend_forward(me, qkv, tables, width):
    quarters, share, _ = qkv.shape
    rows = quarters * share
    padded = jax.ShapeDtypeStruct((rows + WIN, width), BF16)
    return pl.pallas_call(
        forward_kernel,
        out_shape=(
            jax.ShapeDtypeStruct((quarters, share, width), BF16),
            jax.ShapeDtypeStruct((rows, width), BF16),
            padded,
            padded,
        ),
        in_specs=vmem_specs(5),
        out_specs=(pl.BlockSpec(memory_space=pltpu.VMEM),) * 4,
        compiler_params=pltpu.CompilerParams(vmem_limit_bytes=40 * 2**20),
        cost_estimate=pl.CostEstimate(
            flops=16 * rows * WIN * width, bytes_accessed=16 * rows * width, transcendentals=0
        ),
        name="attend_forward",
    )(me, qkv, *tables)


def attend_backward(me, queries, keys, values, grads, tables):
    quarters, share, width = grads.shape
    rows = quarters * share
    accumulator = pltpu.VMEM((rows + WIN, width), F32)
    return pl.pallas_call(
        backward_kernel,
        out_shape=jax.ShapeDtypeStruct((quarters, share, 3 * width), BF16),
        in_specs=vmem_specs(8),
        out_specs=pl.BlockSpec(memory_space=pltpu.VMEM),
        scratch_shapes=[accumulator, accumulator],
        compiler_params=pltpu.CompilerParams(vmem_limit_bytes=40 * 2**20),
        cost_estimate=pl.CostEstimate(
            flops=40 * rows * WIN * width, bytes_accessed=16 * rows * width, transcendentals=0
        ),
        name="attend_backward",
    )(me, queries, keys, values, grads, *tables)


def swap(tensor, bit):
    return lax.ppermute(tensor, "mp", [(i, i ^ bit) for i in range(4)])


def spread(rows):
    across = swap(rows, 2)
    return [rows, swap(rows, 1), across, swap(across, 1)]


def collect(product):
    away = [swap(product(r).astype(BF16), 1) for r in (3, 1)]
    across = swap((product(2) + away[0].astype(F32)).astype(BF16), 2)
    return product(0) + away[1].astype(F32) + across.astype(F32)


def dot_nt(left, right):
    return lax.dot_general(left, right, (((1,), (1,)), ((), ())), preferred_element_type=F32)


def dot_tn(left, right):
    return lax.dot_general(left, right, (((0,), (0,)), ((), ())), preferred_element_type=F32)


def gather_columns(shard):
    parts = lax.all_gather(shard, "dp", axis=0)
    return jnp.transpose(parts, (1, 0, 2)).reshape(shard.shape[0], -1)


def scatter_rows(grad):
    return lax.psum_scatter(grad.astype(BF16), "dp", scatter_dimension=0, tiled=True).astype(F32)


def scatter_columns(grad):
    n = lax.axis_size("dp")
    parts = jnp.transpose(grad.astype(BF16).reshape(grad.shape[0], n, -1), (1, 0, 2))
    return lax.psum_scatter(parts, "dp", scatter_dimension=0, tiled=False).astype(F32)


def body(
    layer_input,
    row_seq,
    qkv_weight,
    out_weight,
    in_weight,
    down_weight,
    attn_gain,
    mlp_gain,
    cotangent,
):
    me = lax.axis_index("mp")
    me_arg = me.reshape(1).astype(jnp.int32)
    share, model = layer_input.shape
    width = qkv_weight.shape[2]
    units = in_weight.shape[2]
    gains = lax.all_gather(jnp.stack([attn_gain, mlp_gain]), "dp", axis=0)
    gains = jnp.transpose(gains, (1, 0, 2)).reshape(2, model).astype(F32)
    gain_one, gain_two = (gains[0], gains[1])
    w_qkv = lax.all_gather(qkv_weight.reshape(-1, 3 * width), "dp", axis=0, tiled=True)
    w_out = gather_columns(out_weight)
    w_in = lax.all_gather(in_weight.reshape(-1, 2 * units), "dp", axis=0, tiled=True)
    w_gate, w_up = (w_in[:, :units], w_in[:, units:])
    w_down = gather_columns(down_weight)

    quarters = jnp.stack(spread(row_seq))
    seq_all = jnp.take(quarters, jnp.arange(4) ^ me, axis=0).reshape(-1)
    group_rows = seq_all.shape[0]
    blocks = group_rows // WIN
    cosine, sine = rotation_tables(positions(seq_all))
    padded_seq = jnp.pad(seq_all, (WIN // 2, WIN // 2), constant_values=-5).reshape(-1, WIN)
    seq_rows = jnp.concatenate([padded_seq[:-1], padded_seq[1:]], axis=1).reshape(
        blocks, 1, 2 * WIN
    )
    tables = (cosine, sine, seq_all[:, None], seq_rows)

    grad_final = cotangent.astype(F32) * (row_seq >= 0).astype(F32)[:, None]
    grad_all = jnp.concatenate(spread(grad_final.astype(BF16)), axis=0)

    block_in = layer_input.astype(F32)
    normed_one, factor_one = normalize(block_in)
    h_all = jnp.concatenate(spread((normed_one * gain_one).astype(BF16)), axis=0)
    qkv = jnp.dot(h_all, w_qkv, preferred_element_type=F32)
    mixed, queries, keys, values = attend_forward(
        me_arg, qkv.reshape(4, share, 3 * width), tables, width
    )
    middle = block_in + collect(
        lambda r: jnp.dot(mixed[r], w_out, preferred_element_type=F32)
    )
    normed_two, factor_two = normalize(middle)
    h2_parts = spread((normed_two * gain_two).astype(BF16))
    h2_all = jnp.concatenate(h2_parts, axis=0)
    gate_vals = jnp.dot(h2_all, w_gate, preferred_element_type=F32)
    up_values = jnp.dot(h2_all, w_up, preferred_element_type=F32)
    hidden = (jax.nn.gelu(gate_vals, approximate=False) * up_values).astype(BF16)

    def quarter_of(tensor, r):
        return lax.slice_in_dim(tensor, r * share, (r + 1) * share, axis=0)

    final_rows = middle + collect(
        lambda r: jnp.dot(quarter_of(hidden, r), w_down, preferred_element_type=F32)
    )
    activations = final_rows.astype(BF16)

    down_share = scatter_columns(dot_tn(hidden, grad_all))
    grad_hidden = dot_nt(grad_all, w_down)

    def product(gate_in, up_in):
        return jax.nn.gelu(gate_in, approximate=False) * up_in

    _, pullback = jax.vjp(product, gate_vals, up_values)
    grad_gate, grad_up = (item.astype(BF16) for item in pullback(grad_hidden))
    grad_h_two = collect(
        lambda r: dot_nt(quarter_of(grad_gate, r), w_gate) + dot_nt(quarter_of(grad_up, r), w_up)
    )
    grad_norm_two, gain_two_grad = norm_back(grad_h_two, normed_two, factor_two, gain_two)
    grad_middle = grad_final + grad_norm_two
    grad_mid_all = jnp.concatenate(spread(grad_middle.astype(BF16)), axis=0)
    in_share = scatter_rows(
        jnp.concatenate([dot_tn(h2_all, grad_gate), dot_tn(h2_all, grad_up)], axis=1)
    ).reshape(-1, 2, units)
    grad_mixed = dot_nt(grad_mid_all, w_out).astype(BF16).reshape(4, share, width)
    grad_qkv = attend_backward(me_arg, queries, keys, values, grad_mixed, tables)
    out_share = scatter_columns(dot_tn(mixed.reshape(group_rows, width), grad_mid_all))
    grad_h_one = collect(lambda r: dot_nt(grad_qkv[r], w_qkv))
    grad_norm_one, gain_one_grad = norm_back(grad_h_one, normed_one, factor_one, gain_one)
    input_grad = (grad_middle + grad_norm_one).astype(BF16)
    qkv_share = scatter_rows(dot_tn(h_all, grad_qkv.reshape(group_rows, 3 * width))).reshape(
        -1, 3, width
    )
    gain_total = lax.psum(jnp.stack([gain_one_grad, gain_two_grad]), ("dp", "mp"))
    own = attn_gain.shape[0]
    gain_total = lax.dynamic_slice_in_dim(gain_total, lax.axis_index("dp") * own, own, 1)
    return (
        activations,
        input_grad,
        gain_total[0],
        gain_total[1],
        qkv_share,
        out_share,
        in_share,
        down_share,
    )


def solution(mesh):
    in_specs = (
        P(("dp", "mp"), None),
        P(("dp", "mp")),
        P("dp", None, "mp"),
        P("mp", "dp"),
        P("dp", None, "mp"),
        P("mp", "dp"),
        P("dp"),
        P("dp"),
        P(("dp", "mp"), None),
    )
    out_specs = (
        P(("dp", "mp"), None),
        P(("dp", "mp"), None),
        P("dp"),
        P("dp"),
        P("dp", None, "mp"),
        P("mp", "dp"),
        P("dp", None, "mp"),
        P("mp", "dp"),
    )
    return jax.shard_map(body, mesh=mesh, in_specs=in_specs, out_specs=out_specs, check_vma=False)
```

time: 1050 us -> 495 us (0.47)
  waiting for transfers between devices: 582 us -> 202 us
  local copies, waits for them, and re-layouts: 107 us -> 22 us
  matrix products: 124 us -> 82.7 us
  other arithmetic: 68.8 us -> 29.4 us
  Pallas kernels: 0 us -> 25.7 us
  loops' own time: 24.3 us -> 0 us
  blocking collectives: 105 us -> 92.6 us
    reduce_scatter x8 -> x3, waiting for transfers between devices: 379 us -> 73.1 us  [the longest x1 65.7 us: scatter_rows(): lax.psum_scatter(grad.astype(BF16), 'dp', scatter_dimension=0, tiled=True)]
    all_gather x7 -> x3, waiting for transfers between devices: 202 us -> 2.61 us  [the longest x1 2.59 us: body(): lax.all_gather(in_weight.reshape(-1, 2 * units), 'dp', axis=0, tiled=True)]
    ppermute x0 -> x27, waiting for transfers between devices: none -> 103 us  [swap(): return lax.ppermute(tensor, 'mp', [(i, i ^ bit) for i in range(4)])]
    dynamic_update_slice x21 -> x0, local copies, waits for them, and re-layouts: 59.8 us -> none  [the longest x6 37.2 us: attend_backward(): lax.scan(one_block, (blank, blank), (offsets, log_totals))]
    dot_general x33 -> x30, matrix products: 124 us -> 82.7 us  [the longest x14 36.9 us: dot_nt(): lax.dot_general(left, right, (((1,), (1,)), ((), ())), preferred_element_...]
    psum x1, blocking collectives: 6.54 us -> 39.9 us  [body(): lax.psum(jnp.stack([gain_one_grad, gain_two_grad]), ('dp', 'mp'))]
    dynamic_slice x36 -> x1, local copies, waits for them, and re-layouts: 27.5 us -> 0.01 us  [body(): lax.dynamic_slice_in_dim(gain_total, lax.axis_index('dp') * own, own, 1)]
    pallas_call x0 -> x2, Pallas kernels: none -> 25.7 us  [the longest x1 14.8 us: attend_backward(): pl.pallas_call(backward_kernel, out_shape=jax.ShapeDtypeStruct((quarters,...]
  transfers between devices with their start and end apart: 15 -> 34, of which waited for: 14 -> 12; matrix products, arithmetic and copies ran while one was open for 6% -> 20% of each run, Pallas kernels for 0% -> 5%
where the time goes in v1:
time: 495 us; the launch traced here: 487 us
  waiting for transfers between devices  202 us (41%)
  blocking collectives  92.6 us (19%)
  matrix products  82.7 us (17%)
  other arithmetic  29.4 us (6%)
  Pallas kernels  25.7 us (5%)
  local copies, waits for them, and re-layouts  22 us (4%)
  starting transfers between devices  16.8 us (3%)
  between operations  15.4 us (3%)
    ppermute x27, waiting for transfers between devices, swap(): return lax.ppermute(tensor, 'mp', [(i, i ^ bit) for i in range(4)])  103 us
    reduce_scatter x1, waiting for transfers between devices, scatter_rows(): lax.psum_scatter(grad.astype(BF16), 'dp', scatter_dimension=0, tiled=True)  65.7 us
    psum x1, blocking collectives, body(): lax.psum(jnp.stack([gain_one_grad, gain_two_grad]), ('dp', 'mp'))  39.9 us
    dot_general x14, matrix products, dot_nt(): lax.dot_general(left, right, (((1,), (1,)), ((), ())), preferred_element_...  36.9 us
    all_gather x1, blocking collectives, gather_columns(): parts = lax.all_gather(shard, 'dp', axis=0)  32.1 us
    unnamed x8, waiting for transfers between devices  23.3 us
    all_gather x1, blocking collectives, body(): gains = lax.all_gather(jnp.stack([attn_gain, mlp_gain]), 'dp', axis=0)  20.7 us
    dot_general x5, matrix products, dot_tn(): lax.dot_general(left, right, (((0,), (0,)), ((), ())), preferred_element_...  19.9 us
  transfers between devices with their start and end apart: 34, of which 12 were waited for; matrix products, arithmetic and copies ran while one was open for 20% of the time, Pallas kernels for 5%

profile of v1, /device:TPU:0, one launch (start us, length us, event | category | flops | bytes accessed | tf_op | source)
XLA Modules:
  0.0 486.7 jit_solution(13230116549434259937)
XLA Ops:
  12.9 20.7 %all-gather.3 = bf16[8,2,128]{2,1,0:T(2,128)(2,1)S(1)} all-gather(bf16[1,2,128]{2,1,0:T(2,128)(2,1)S(1)} %maximum_bitcast_fusion), channel_id=2, replica_groups=mesh['dp'=8,'mp'=4] {'dp'}, dimensions={0}, use_global_device_ids=true | all-gather | bytes 4608 | tf_op jit(solution)/shard_map/all_gather | solution.py:297
  37.5 32.1 %all-gather.1 = bf16[2048,128]{1,0:T(8,128)(2,1)S(1)} all-gather(bf16[256,128]{1,0:T(8,128)(2,1)S(1)} %copy-done.25), channel_id=3, replica_groups=mesh['dp'=8,'mp'=4] {'dp'}, dimensions={0}, use_global_device_ids=true | all-gather | bytes 589824 | tf_op jit(solution)/shard_map/all_gather | solution.py:267
  73.3 2.8 fusion.70
  77.5 5.9 %fusion.57 = f32[1536,768]{1,0:T(8,128)S(1)} fusion(bf16[1024,768]{0,1:T(8,128)(2,1)} %all-gather.8.cloned.1.call-done, bf16[384,1024]{1,0:T(8,128)(2,1)} %collective-permute-done.2, bf16[384,1024]{1,0:T(8,128)(2,1)} %collective-permute-done.1, bf16[384,1024]{1,0:T(8,128)(2,1)} %collective-permute-done, bf16[384,1024]{1,0:T(8,128)(2,1)S(1)} %fusion.12), kind=kOutput, calls=%fused_computation.116 | convolution fusion | flops 2428502016 | bytes 9437184 | tf_op jit(solution)/shard_map/dot_general | solution.py:323
  83.4 10.9 %attend_forward.1 = (bf16[4,384,256]{2,1,0:T(8,128)(2,1)S(1)}, bf16[1536,256]{1,0:T(8,128)(2,1)S(1)}, bf16[1664,256]{1,0:T(8,128)(2,1)S(1)}, bf16[1664,256]{1,0:T(8,128)(2,1)S(1)}) custom-call(s32[1]{0:T(128)} %bitcast.me_ref, f32[4,384,768]{2,1,0:T(8,128)S(1)} %bitcast.136, f32[1536,128]{1,0:T(8,128)S(1)} %get-tuple-element.83.cos_ref, ...), custom_call_target="tpu_custom_call" | custom-call | flops 805306368 | bytes 6291456 | tf_op jit(solution)/shard_map/attend_forward/pallas_call | solution.py:207
  105.8 16.6 %collective-permute-done.8 = bf16[384,1024]{1,0:T(8,128)(2,1)S(1)} collective-permute-done((bf16[384,1024]{1,0:T(8,128)(2,1)S(1)}, bf16[384,1024]{1,0:T(8,128)(2,1)S(1)}, u32[]{:S(2)}, u32[]{:S(2)}) %collective-permute-start.8) | collective-permute-done | bytes 786464 | tf_op jit(solution)/shard_map/ppermute | solution.py:244
  127.4 17.7 %collective-permute-done.10 = bf16[384,1024]{1,0:T(8,128)(2,1)} collective-permute-done((bf16[384,1024]{1,0:T(8,128)(2,1)}, bf16[384,1024]{1,0:T(8,128)(2,1)}, u32[]{:S(2)}, u32[]{:S(2)}) %collective-permute-start.10) | collective-permute-done | bytes 786464 | tf_op jit(solution)/shard_map/ppermute | solution.py:244
  145.6 14.6 %collective-permute-done.16 = bf16[384,1024]{1,0:T(8,128)(2,1)} collective-permute-done((bf16[384,1024]{1,0:T(8,128)(2,1)}, bf16[384,1024]{1,0:T(8,128)(2,1)}, u32[]{:S(2)}, u32[]{:S(2)}) %collective-permute-start.16) | collective-permute-done | bytes 786464 | tf_op jit(solution)/shard_map/ppermute | solution.py:244
  160.2 2.8 copy.50
  165.6 4.7 fusion.53
  170.3 4.2 fusion.43
  174.6 14.3 %multiply_convert_fusion = (bf16[1536,656]{0,1:T(8,128)(2,1)}, f32[1536,656]{0,1:T(8,128)S(1)}, f32[1536,656]{0,1:T(8,128)S(1)}) fusion(f32[1536,656]{0,1:T(8,128)S(1)} %fusion.53, bf16[82,8,8,128]{3,2,1,0:T(8,128)(2,1)S(1)} %bitcast.150, bf16[384,1024]{1,0:T(8,128)(2,1)} %collective-permute-done.17, bf16[384,1024]{1,0:T(8,128)(2,1)} %collective-permute-done.16, ...), kind=kOutput, calls=%fused_computation.3 | convolution fusion | flops 2142683136 | bytes 18595840 | tf_op jit(solution)/shard_map/dot_general | solution.py:259
  188.9 3.2 add_convert_fusion
  195.5 4.1 fusion.21
  217.0 15.9 %collective-permute-done.20 = bf16[384,1024]{1,0:T(8,128)(2,1)S(1)} collective-permute-done((bf16[384,1024]{1,0:T(8,128)(2,1)S(1)}, bf16[384,1024]{1,0:T(8,128)(2,1)S(1)}, u32[]{:S(2)}, u32[]{:S(2)}) %collective-permute-start.20) | collective-permute-done | bytes 786464 | tf_op jit(solution)/shard_map/ppermute | solution.py:244
  233.9 14.7 %collective-permute-done.14 = bf16[384,1024]{1,0:T(8,128)(2,1)S(1)} collective-permute-done((bf16[384,1024]{1,0:T(8,128)(2,1)S(1)}, bf16[384,1024]{1,0:T(8,128)(2,1)S(1)}, u32[]{:S(2)}, u32[]{:S(2)}) %collective-permute-start.14) | collective-permute-done | bytes 786464 | tf_op jit(solution)/shard_map/ppermute | solution.py:244
  252.5 16.9 %collective-permute-done.22 = bf16[384,1024]{1,0:T(8,128)(2,1)S(1)} collective-permute-done((bf16[384,1024]{1,0:T(8,128)(2,1)S(1)}, bf16[384,1024]{1,0:T(8,128)(2,1)S(1)}, u32[]{:S(2)}, u32[]{:S(2)}) %collective-permute-start.22) | collective-permute-done | bytes 786464 | tf_op jit(solution)/shard_map/ppermute | solution.py:244
  274.0 4.8 convolution_convert_fusion.3
  278.8 4.2 convolution_convert_fusion.2
  284.8 4.5 copy.56
  289.7 3.1 convolution_convert_fusion
  292.8 14.8 %attend_backward.1 = bf16[4,384,768]{2,1,0:T(8,128)(2,1)S(1)} custom-call(s32[1]{0:T(128)} %bitcast.me_ref, bf16[1536,256]{1,0:T(8,128)(2,1)S(1)} %copy-done.5, bf16[1664,256]{1,0:T(8,128)(2,1)S(1)} %get-tuple-element.14.k_ref, bf16[1664,256]{1,0:T(8,128)(2,1)S(1)} %copy-done.3, bf16[4,384,256]{2,1,0:T(8,128)(2,1)S(1)} %bitcast.138, ...), custom_call_target="tpu_custom_call" | custom-call | flops 2013265920 | bytes 6291456 | tf_op jit(solution)/shard_map/attend_backward/pallas_call | solution.py:229
  309.5 5.5 %convolution_convert_fusion.1 = bf16[1024,768]{1,0:T(8,128)(2,1)} fusion(bf16[1536,768]{1,0:T(8,128)(2,1)S(1)} %bitcast.137, bf16[384,1024]{1,0:T(8,128)(2,1)} %collective-permute-done.2, bf16[384,1024]{1,0:T(8,128)(2,1)} %collective-permute-done.1, bf16[384,1024]{1,0:T(8,128)(2,1)} %collective-permute-done, bf16[384,1024]{1,0:T(8,128)(2,1)S(1)} %copy-done.24), kind=kOutput, calls=%fused_computation.35 | convolution fusion | flops 2429288448 | bytes 7077888 | tf_op jit(solution)/shard_map/dot_general | solution.py:263
  315.0 3.4 convolution_convert_fusion.6
  323.7 3.4 fusion.56
  327.2 7.4 %reduce-scatter.9.cloned.1.call-done = bf16[1,256,128]{2,1,0:T(8,128)(2,1)} async-done(((bf16[8,256,128]{2,1,0:T(8,128)(2,1)}), bf16[1,256,128]{2,1,0:T(8,128)(2,1)}) %reduce-scatter.9.cloned.1.call-update) | async-done | bytes 65552 | tf_op jit(solution)/shard_map/reduce_scatter | solution.py:278
  336.1 4.3 collective-permute-done.26
  340.4 2.7 fusion.18
  343.1 39.9 %psum.7 = f32[2,1024]{1,0:T(2,128)S(1)} all-reduce(f32[2,1024]{1,0:T(2,128)S(1)} %pad_maximum_fusion.13), channel_id=1, replica_groups=mesh['dp'=8,'mp'=4] {'dp','mp'}, use_global_device_ids=true, to_apply=%region_12.13 | all-reduce | flops 2048 | bytes 16384 | tf_op jit(solution)/shard_map/psum | solution.py:371
  383.5 2.9 fusion.17
  386.4 23.2 %reduce-scatter.13.cloned.1.call-done = bf16[128,1312]{1,0:T(8,128)(2,1)} async-done(((bf16[1024,1312]{1,0:T(8,128)(2,1)}), bf16[128,1312]{1,0:T(8,128)(2,1)}) %reduce-scatter.13.cloned.1.call-update) | async-done | bytes 335888
  411.7 65.7 %reduce-scatter.7.cloned.1.call-done = bf16[128,768]{1,0:T(8,128)(2,1)} async-done(((bf16[1024,768]{1,0:T(8,128)(2,1)}), bf16[128,768]{1,0:T(8,128)(2,1)}) %reduce-scatter.7.cloned.1.call-update) | async-done | bytes 196624 | tf_op jit(solution)/shard_map/reduce_scatter | solution.py:272
  (231 shorter events, 79.3 us)
Async XLA Ops:
  7.2 70.2 %all-gather.8.cloned.1.call-start = ((), (), s32[]{:S(2)}) async-start(), calls=%async_computation.4 | async-start | bytes 1769472 | tf_op jit(solution)/shard_map/all_gather | solution.py:300
  9.1 151.1 %all-gather.12.cloned.1.call-start = ((), (), s32[]{:S(2)}) async-start(), calls=%async_computation.9 | async-start | bytes 1511424 | tf_op jit(solution)/shard_map/all_gather | solution.py:267
  9.1 61.8 %collective-permute-start.3 = (s32[384]{0:T(512)}, s32[384]{0:T(512)S(1)}, u32[]{:S(2)}, u32[]{:S(2)}) collective-permute-start(s32[384]{0:T(512)} %param.10), channel_id=1, source_target_pairs={{0,1},{1,0},{2,3},{3,2},{4,5},{5,4},{6,7},{7,6},{8,9},{9,8},{10,11... | collective-permute-start | bytes 4616 | tf_op jit(solution)/shard_map/ppermute | solution.py:244
  9.6 60.0 %collective-permute-start.4 = (s32[384]{0:T(512)}, s32[384]{0:T(512)S(1)}, u32[]{:S(2)}, u32[]{:S(2)}) collective-permute-start(s32[384]{0:T(512)} %param.10), channel_id=1, source_target_pairs={{0,2},{1,3},{2,0},{3,1},{4,6},{5,7},{6,4},{7,5},{8,10},{9,11},{10,... | collective-permute-start | bytes 4616 | tf_op jit(solution)/shard_map/ppermute | solution.py:244
  36.8 36.0 %collective-permute-start.1 = (bf16[384,1024]{1,0:T(8,128)(2,1)S(1)}, bf16[384,1024]{1,0:T(8,128)(2,1)}, u32[]{:S(2)}, u32[]{:S(2)}) collective-permute-start(bf16[384,1024]{1,0:T(8,128)(2,1)S(1)} %fusion.12), channel_id=1, source_target_pairs={{0,2},{1,3},{2,0},{3,1},{4,6},{5,7},{6,4},{7,5},{8,10},{9,11},{10,... | collective-permute-start | bytes 2359304 | tf_op jit(solution)/shard_map/ppermute | solution.py:244
  37.4 40.0 %collective-permute-start = (bf16[384,1024]{1,0:T(8,128)(2,1)S(1)}, bf16[384,1024]{1,0:T(8,128)(2,1)}, u32[]{:S(2)}, u32[]{:S(2)}) collective-permute-start(bf16[384,1024]{1,0:T(8,128)(2,1)S(1)} %fusion.12), channel_id=1, source_target_pairs={{0,1},{1,0},{2,3},{3,2},{4,5},{5,4},{6,7},{7,6},{8,9},{9,8},{10,11... | collective-permute-start | bytes 2359304 | tf_op jit(solution)/shard_map/ppermute | solution.py:244
  37.4 128.1 %all-gather.10.cloned.1.call-start = ((), (), s32[]{:S(2)}) async-start(), calls=%async_computation.5 | async-start | bytes 3022848 | tf_op jit(solution)/shard_map/all_gather | solution.py:302
  72.8 4.6 collective-permute-start.2
  98.3 2.8 collective-permute-start.7
  98.3 223.8 %reduce-scatter.11.cloned.1.call-start = ((), (), s32[]{:S(2)}) async-start(), calls=%async_computation.8 | async-start | bytes 1511424 | tf_op jit(solution)/shard_map/reduce_scatter | solution.py:278
  100.5 5.3 %collective-permute-start.6 = (bf16[384,1024]{1,0:T(8,128)(2,1)S(1)}, bf16[384,1024]{1,0:T(8,128)(2,1)S(1)}, u32[]{:S(2)}, u32[]{:S(2)}) collective-permute-start(bf16[384,1024]{1,0:T(8,128)(2,1)S(1)} %convolution_convert_fusion.10), channel_id=1, source_target_pairs={{0,1},{1,0},{2,3},{3,2},{4,5},{5,4},{6,7},{7,6},{8,9},{9,8},{10,11... | collective-permute-start | bytes 2359304 | tf_op jit(solution)/shard_map/ppermute | solution.py:244
  102.8 19.5 %collective-permute-start.8 = (bf16[384,1024]{1,0:T(8,128)(2,1)S(1)}, bf16[384,1024]{1,0:T(8,128)(2,1)S(1)}, u32[]{:S(2)}, u32[]{:S(2)}) collective-permute-start(bf16[384,1024]{1,0:T(8,128)(2,1)S(1)} %add_convert_fusion.7), channel_id=1, source_target_pairs={{0,2},{1,3},{2,0},{3,1},{4,6},{5,7},{6,4},{7,5},{8,10},{9,11},{10,... | collective-permute-start | bytes 2359304 | tf_op jit(solution)/shard_map/ppermute | solution.py:244
  124.3 20.8 %collective-permute-start.10 = (bf16[384,1024]{1,0:T(8,128)(2,1)}, bf16[384,1024]{1,0:T(8,128)(2,1)}, u32[]{:S(2)}, u32[]{:S(2)}) collective-permute-start(bf16[384,1024]{1,0:T(8,128)(2,1)} %multiply_convert_fusion.2), channel_id=1, source_target_pairs={{0,2},{1,3},{2,0},{3,1},{4,6},{5,7},{6,4},{7,5},{8,10},{9,11},{10,... | collective-permute-start | bytes 2359304 | tf_op jit(solution)/shard_map/ppermute | solution.py:244
  126.9 33.3 %collective-permute-start.16 = (bf16[384,1024]{1,0:T(8,128)(2,1)}, bf16[384,1024]{1,0:T(8,128)(2,1)}, u32[]{:S(2)}, u32[]{:S(2)}) collective-permute-start(bf16[384,1024]{1,0:T(8,128)(2,1)} %fusion.20), channel_id=1, source_target_pairs={{0,2},{1,3},{2,0},{3,1},{4,6},{5,7},{6,4},{7,5},{8,10},{9,11},{10,... | collective-permute-start | bytes 2359304 | tf_op jit(solution)/shard_map/ppermute | solution.py:244
  127.4 38.2 %collective-permute-start.9 = (bf16[384,1024]{1,0:T(8,128)(2,1)}, bf16[384,1024]{1,0:T(8,128)(2,1)}, u32[]{:S(2)}, u32[]{:S(2)}) collective-permute-start(bf16[384,1024]{1,0:T(8,128)(2,1)} %multiply_convert_fusion.2), channel_id=1, source_target_pairs={{0,1},{1,0},{2,3},{3,2},{4,5},{5,4},{6,7},{7,6},{8,9},{9,8},{10,11... | collective-permute-start | bytes 2359304 | tf_op jit(solution)/shard_map/ppermute | solution.py:244
  145.1 20.5 %collective-permute-start.11 = (bf16[384,1024]{1,0:T(8,128)(2,1)}, bf16[384,1024]{1,0:T(8,128)(2,1)}, u32[]{:S(2)}, u32[]{:S(2)}) collective-permute-start(bf16[384,1024]{1,0:T(8,128)(2,1)} %collective-permute-done.10), channel_id=1, source_target_pairs={{0,1},{1,0},{2,3},{3,2},{4,5},{5,4},{6,7},{7,6},{8,9},{9,8},{10,11... | collective-permute-start | bytes 2359304 | tf_op jit(solution)/shard_map/ppermute | solution.py:244
  145.1 29.4 %collective-permute-start.15 = (bf16[384,1024]{1,0:T(8,128)(2,1)}, bf16[384,1024]{1,0:T(8,128)(2,1)}, u32[]{:S(2)}, u32[]{:S(2)}) collective-permute-start(bf16[384,1024]{1,0:T(8,128)(2,1)} %fusion.20), channel_id=1, source_target_pairs={{0,1},{1,0},{2,3},{3,2},{4,5},{5,4},{6,7},{7,6},{8,9},{9,8},{10,11... | collective-permute-start | bytes 2359304 | tf_op jit(solution)/shard_map/ppermute | solution.py:244
  160.2 14.3 %collective-permute-start.17 = (bf16[384,1024]{1,0:T(8,128)(2,1)}, bf16[384,1024]{1,0:T(8,128)(2,1)}, u32[]{:S(2)}, u32[]{:S(2)}) collective-permute-start(bf16[384,1024]{1,0:T(8,128)(2,1)} %collective-permute-done.16), channel_id=1, source_target_pairs={{0,1},{1,0},{2,3},{3,2},{4,5},{5,4},{6,7},{7,6},{8,9},{9,8},{10,11... | collective-permute-start | bytes 2359304 | tf_op jit(solution)/shard_map/ppermute | solution.py:244
  201.1 133.5 %reduce-scatter.9.cloned.1.call-start = ((), (), s32[]{:S(2)}) async-start(), calls=%async_computation.7 | async-start | bytes 589824 | tf_op jit(solution)/shard_map/reduce_scatter | solution.py:278
  201.3 32.6 %collective-permute-start.12 = (bf16[384,1024]{1,0:T(8,128)(2,1)}, bf16[384,1024]{1,0:T(8,128)(2,1)S(1)}, u32[]{:S(2)}, u32[]{:S(2)}) collective-permute-start(bf16[384,1024]{1,0:T(8,128)(2,1)} %convolution_convert_fusion.8), channel_id=1, source_target_pairs={{0,1},{1,0},{2,3},{3,2},{4,5},{5,4},{6,7},{7,6},{8,9},{9,8},{10,11... | collective-permute-start | bytes 2359304 | tf_op jit(solution)/shard_map/ppermute | solution.py:244
  201.4 14.2 %collective-permute-start.13 = (bf16[384,1024]{1,0:T(8,128)(2,1)}, bf16[384,1024]{1,0:T(8,128)(2,1)S(1)}, u32[]{:S(2)}, u32[]{:S(2)}) collective-permute-start(bf16[384,1024]{1,0:T(8,128)(2,1)} %convolution_convert_fusion.7), channel_id=1, source_target_pairs={{0,1},{1,0},{2,3},{3,2},{4,5},{5,4},{6,7},{7,6},{8,9},{9,8},{10,11... | collective-permute-start | bytes 2359304 | tf_op jit(solution)/shard_map/ppermute | solution.py:244
  206.4 5.1 %collective-permute-start.19 = (bf16[384,1024]{1,0:T(8,128)(2,1)S(1)}, bf16[384,1024]{1,0:T(8,128)(2,1)S(1)}, u32[]{:S(2)}, u32[]{:S(2)}) collective-permute-start(bf16[384,1024]{1,0:T(8,128)(2,1)S(1)} %add_convert_fusion.3), channel_id=1, source_target_pairs={{0,1},{1,0},{2,3},{3,2},{4,5},{5,4},{6,7},{7,6},{8,9},{9,8},{10,11... | collective-permute-start | bytes 2359304 | tf_op jit(solution)/shard_map/ppermute | solution.py:244
  208.8 8.2 %collective-permute-start.18 = (bf16[384,1024]{1,0:T(8,128)(2,1)S(1)}, bf16[384,1024]{1,0:T(8,128)(2,1)S(1)}, u32[]{:S(2)}, u32[]{:S(2)}) collective-permute-start(bf16[384,1024]{1,0:T(8,128)(2,1)S(1)} %add_convert_fusion.4), channel_id=1, source_target_pairs={{0,1},{1,0},{2,3},{3,2},{4,5},{5,4},{6,7},{7,6},{8,9},{9,8},{10,11... | collective-permute-start | bytes 2359304 | tf_op jit(solution)/shard_map/ppermute | solution.py:244
  212.4 20.5 %collective-permute-start.20 = (bf16[384,1024]{1,0:T(8,128)(2,1)S(1)}, bf16[384,1024]{1,0:T(8,128)(2,1)S(1)}, u32[]{:S(2)}, u32[]{:S(2)}) collective-permute-start(bf16[384,1024]{1,0:T(8,128)(2,1)S(1)} %add_convert_fusion.2), channel_id=1, source_target_pairs={{0,2},{1,3},{2,0},{3,1},{4,6},{5,7},{6,4},{7,5},{8,10},{9,11},{10,... | collective-permute-start | bytes 2359304 | tf_op jit(solution)/shard_map/ppermute | solution.py:244
  216.4 32.2 %collective-permute-start.14 = (bf16[384,1024]{1,0:T(8,128)(2,1)S(1)}, bf16[384,1024]{1,0:T(8,128)(2,1)S(1)}, u32[]{:S(2)}, u32[]{:S(2)}) collective-permute-start(bf16[384,1024]{1,0:T(8,128)(2,1)S(1)} %add_convert_fusion.6), channel_id=1, source_target_pairs={{0,2},{1,3},{2,0},{3,1},{4,6},{5,7},{6,4},{7,5},{8,10},{9,11},{10,... | collective-permute-start | bytes 2359304 | tf_op jit(solution)/shard_map/ppermute | solution.py:244
  250.9 18.5 %collective-permute-start.22 = (bf16[384,1024]{1,0:T(8,128)(2,1)S(1)}, bf16[384,1024]{1,0:T(8,128)(2,1)S(1)}, u32[]{:S(2)}, u32[]{:S(2)}) collective-permute-start(bf16[384,1024]{1,0:T(8,128)(2,1)S(1)} %get-tuple-element.63), channel_id=1, source_target_pairs={{0,2},{1,3},{2,0},{3,1},{4,6},{5,7},{6,4},{7,5},{8,10},{9,11},{10,... | collective-permute-start | bytes 2359304 | tf_op jit(solution)/shard_map/ppermute | solution.py:244
  252.5 16.9 %collective-permute-start.21 = (bf16[384,1024]{1,0:T(8,128)(2,1)S(1)}, bf16[384,1024]{1,0:T(8,128)(2,1)S(1)}, u32[]{:S(2)}, u32[]{:S(2)}) collective-permute-start(bf16[384,1024]{1,0:T(8,128)(2,1)S(1)} %get-tuple-element.63), channel_id=1, source_target_pairs={{0,1},{1,0},{2,3},{3,2},{4,5},{5,4},{6,7},{7,6},{8,9},{9,8},{10,11... | collective-permute-start | bytes 2359304 | tf_op jit(solution)/shard_map/ppermute | solution.py:244
  273.9 135.7 %reduce-scatter.13.cloned.1.call-start = ((), (), s32[]{:S(2)}) async-start(), calls=%async_computation.10 | async-start | bytes 3244032
  289.3 188.0 %reduce-scatter.7.cloned.1.call-start = ((), (), s32[]{:S(2)}) async-start(), calls=%async_computation.6 | async-start | bytes 1769472 | tf_op jit(solution)/shard_map/reduce_scatter | solution.py:272
  309.3 9.5 %collective-permute-start.25 = (bf16[384,1024]{1,0:T(8,128)(2,1)}, bf16[384,1024]{1,0:T(8,128)(2,1)S(1)}, u32[]{:S(2)}, u32[]{:S(2)}) collective-permute-start(bf16[384,1024]{1,0:T(8,128)(2,1)} %convolution_convert_fusion.5), channel_id=1, source_target_pairs={{0,1},{1,0},{2,3},{3,2},{4,5},{5,4},{6,7},{7,6},{8,9},{9,8},{10,11... | collective-permute-start | bytes 2359304 | tf_op jit(solution)/shard_map/ppermute | solution.py:244
  318.4 17.6 %collective-permute-start.24 = (bf16[384,1024]{1,0:T(8,128)(2,1)}, bf16[384,1024]{1,0:T(8,128)(2,1)}, u32[]{:S(2)}, u32[]{:S(2)}) collective-permute-start(bf16[384,1024]{1,0:T(8,128)(2,1)} %convolution_convert_fusion.6), channel_id=1, source_target_pairs={{0,1},{1,0},{2,3},{3,2},{4,5},{5,4},{6,7},{7,6},{8,9},{9,8},{10,11... | collective-permute-start | bytes 2359304 | tf_op jit(solution)/shard_map/ppermute | solution.py:244
  320.5 19.9 %collective-permute-start.26 = (bf16[384,1024]{1,0:T(8,128)(2,1)}, bf16[384,1024]{1,0:T(8,128)(2,1)}, u32[]{:S(2)}, u32[]{:S(2)}) collective-permute-start(bf16[384,1024]{1,0:T(8,128)(2,1)} %add_convert_fusion.1), channel_id=1, source_target_pairs={{0,2},{1,3},{2,0},{3,1},{4,6},{5,7},{6,4},{7,5},{8,10},{9,11},{10,... | collective-permute-start | bytes 2359304 | tf_op jit(solution)/shard_map/ppermute | solution.py:244
  (44 other events, 557.7 us)
Sparse Core Ops, SparseCore 0:
  10.7 51.9 all-gather.7
  64.9 42.2 all-gather.11
  109.2 56.3 all-gather.9
  201.2 59.8 reduce-scatter.10
  274.0 60.4 reduce-scatter.8
  338.4 71.1 reduce-scatter.12
  413.4 63.9 reduce-scatter.6

commit v2 on v1

--- a/solution.py
+++ b/solution.py
@@ -97,11 +97,13 @@
     return (stacked, weights * (1.0 / total))
 
 
-def forward_kernel(me_ref, qkv_ref, cos_ref, sin_ref, col_ref, row_ref, o_ref, q_ref, k_ref, v_ref):
+def forward_kernel(
+    me_ref, qi_ref, ki_ref, vi_ref, cos_ref, sin_ref, col_ref, row_ref, o_ref, q_ref, k_ref, v_ref
+):
     me = me_ref[0]
     rows, width = q_ref.shape
     blocks = rows // WIN
-    per_quarter = qkv_ref.shape[1] // WIN
+    per_quarter = qi_ref.shape[1] // WIN
     half = WIN // 2
     for ref in (k_ref, v_ref):
         ref[0:half, :] = jnp.zeros((half, width), BF16)
@@ -113,9 +115,9 @@
         here = pl.ds(start, WIN)
         later = pl.ds(pl.multiple_of(start + half, half), WIN)
         cosine, sine = (cos_ref[here, :], sin_ref[here, :])
-        q_ref[here, :] = turn(qkv_ref[quarter, inner, 0:width], cosine, sine).astype(BF16)
-        k_ref[later, :] = turn(qkv_ref[quarter, inner, width : 2 * width], cosine, sine).astype(BF16)
-        v_ref[later, :] = qkv_ref[quarter, inner, 2 * width : 3 * width].astype(BF16)
+        q_ref[here, :] = turn(qi_ref[quarter, inner, :], cosine, sine).astype(BF16)
+        k_ref[later, :] = turn(ki_ref[quarter, inner, :], cosine, sine).astype(BF16)
+        v_ref[later, :] = vi_ref[quarter, inner, :].astype(BF16)
         return carry
 
     lax.fori_loop(0, blocks, turn_block, 0)
@@ -200,8 +202,8 @@
     return [pl.BlockSpec(memory_space=pltpu.SMEM)] + [pl.BlockSpec(memory_space=pltpu.VMEM)] * count
 
 
-def attend_forward(me, qkv, tables, width):
-    quarters, share, _ = qkv.shape
+def attend_forward(me, qkv, tables):
+    quarters, share, width = qkv[0].shape
     rows = quarters * share
     padded = jax.ShapeDtypeStruct((rows + WIN, width), BF16)
     return pl.pallas_call(
@@ -212,14 +214,14 @@
             padded,
             padded,
         ),
-        in_specs=vmem_specs(5),
+        in_specs=vmem_specs(7),
         out_specs=(pl.BlockSpec(memory_space=pltpu.VMEM),) * 4,
         compiler_params=pltpu.CompilerParams(vmem_limit_bytes=40 * 2**20),
         cost_estimate=pl.CostEstimate(
             flops=16 * rows * WIN * width, bytes_accessed=16 * rows * width, transcendentals=0
         ),
         name="attend_forward",
-    )(me, qkv, *tables)
+    )(me, *qkv, *tables)
 
 
 def attend_backward(me, queries, keys, values, grads, tables):
@@ -263,19 +265,70 @@
     return lax.dot_general(left, right, (((0,), (0,)), ((), ())), preferred_element_type=F32)
 
 
-def gather_columns(shard):
-    parts = lax.all_gather(shard, "dp", axis=0)
-    return jnp.transpose(parts, (1, 0, 2)).reshape(shard.shape[0], -1)
+def pairs(bit):
+    return [(i, i ^ bit) for i in range(lax.axis_size("dp"))]
+
+
+def dp_bits():
+    bits = []
+    while 2 ** len(bits) < lax.axis_size("dp"):
+        bits.insert(0, 2 ** len(bits))
+    return bits
+
+
+def my_bit(bit):
+    return (lax.axis_index("dp") & bit) != 0
+
+
+def first_doublings(shard):
+    held = shard
+    for step, bit in enumerate(dp_bits()[:-1]):
+        held = doubling(held, step, bit)
+    return held
+
+
+def doubling(held, step, bit):
+    other = lax.ppermute(held, "dp", pairs(bit))
+    upper = my_bit(bit)
+    return jnp.stack(
+        [jnp.where(upper, other, held), jnp.where(upper, held, other)], axis=step
+    )
+
+
+def last_doubling(held, shard_shape):
+    bits = dp_bits()
+    return doubling(held, len(bits) - 1, bits[-1]).reshape((-1,) + shard_shape)
+
+
+def halving(parts):
+    bits = dp_bits()
+    held = parts.reshape((2,) * len(bits) + parts.shape[1:])
+    for step in reversed(range(len(bits))):
+        mine = my_bit(bits[step]).astype(jnp.int32)
+        away = lax.dynamic_index_in_dim(held, 1 - mine, axis=step, keepdims=False)
+        kept = lax.dynamic_index_in_dim(held, mine, axis=step, keepdims=False)
+        arrived = lax.ppermute(away, "dp", pairs(bits[step]))
+        held = (kept.astype(F32) + arrived.astype(F32)).astype(
+            parts.dtype if step else F32
+        )
+    return held
+
+
+def merge_rows(parts):
+    return parts.reshape((-1,) + parts.shape[2:])
+
+
+def merge_columns(parts):
+    return jnp.transpose(parts, (1, 0, 2)).reshape(parts.shape[1], -1)
 
 
 def scatter_rows(grad):
-    return lax.psum_scatter(grad.astype(BF16), "dp", scatter_dimension=0, tiled=True).astype(F32)
+    return halving(grad.astype(BF16).reshape(lax.axis_size("dp"), -1, grad.shape[1]))
 
 
 def scatter_columns(grad):
-    n = lax.axis_size("dp")
-    parts = jnp.transpose(grad.astype(BF16).reshape(grad.shape[0], n, -1), (1, 0, 2))
-    return lax.psum_scatter(parts, "dp", scatter_dimension=0, tiled=False).astype(F32)
+    parts = grad.astype(BF16).reshape(grad.shape[0], lax.axis_size("dp"), -1)
+    return halving(jnp.transpose(parts, (1, 0, 2)))
 
 
 def body(
@@ -294,14 +347,21 @@
     share, model = layer_input.shape
     width = qkv_weight.shape[2]
     units = in_weight.shape[2]
-    gains = lax.all_gather(jnp.stack([attn_gain, mlp_gain]), "dp", axis=0)
-    gains = jnp.transpose(gains, (1, 0, 2)).reshape(2, model).astype(F32)
+    gain_shape = (2,) + attn_gain.shape
+    gains = last_doubling(first_doublings(jnp.stack([attn_gain, mlp_gain])), gain_shape)
+    gains = merge_columns(gains).astype(F32)
     gain_one, gain_two = (gains[0], gains[1])
-    w_qkv = lax.all_gather(qkv_weight.reshape(-1, 3 * width), "dp", axis=0, tiled=True)
-    w_out = gather_columns(out_weight)
-    w_in = lax.all_gather(in_weight.reshape(-1, 2 * units), "dp", axis=0, tiled=True)
-    w_gate, w_up = (w_in[:, :units], w_in[:, units:])
-    w_down = gather_columns(down_weight)
+    x_parts = spread(layer_input)
+    projections = [first_doublings(qkv_weight[:, part]) for part in range(3)]
+    late = [out_weight, in_weight[:, 0], in_weight[:, 1], down_weight]
+    *late, projections[2] = lax.optimization_barrier((*late, projections[2]))
+    w_q, w_k, w_v = [
+        merge_rows(last_doubling(item, (qkv_weight.shape[0], width))) for item in projections
+    ]
+    late = [last_doubling(first_doublings(item), item.shape) for item in late]
+    w_out, w_down = (merge_columns(late[0]), merge_columns(late[3]))
+    w_gate, w_up = (merge_rows(late[1]), merge_rows(late[2]))
+    w_qkv = jnp.concatenate([w_q, w_k, w_v], axis=1)
 
     quarters = jnp.stack(spread(row_seq))
     seq_all = jnp.take(quarters, jnp.arange(4) ^ me, axis=0).reshape(-1)
@@ -315,62 +375,85 @@
     tables = (cosine, sine, seq_all[:, None], seq_rows)
 
     grad_final = cotangent.astype(F32) * (row_seq >= 0).astype(F32)[:, None]
-    grad_all = jnp.concatenate(spread(grad_final.astype(BF16)), axis=0)
+    grad_parts = spread(grad_final.astype(BF16))
 
     block_in = layer_input.astype(F32)
     normed_one, factor_one = normalize(block_in)
-    h_all = jnp.concatenate(spread((normed_one * gain_one).astype(BF16)), axis=0)
-    qkv = jnp.dot(h_all, w_qkv, preferred_element_type=F32)
-    mixed, queries, keys, values = attend_forward(
-        me_arg, qkv.reshape(4, share, 3 * width), tables, width
-    )
+    h_all = (normalize(jnp.concatenate(x_parts, axis=0).astype(F32))[0] * gain_one).astype(BF16)
+    qkv = [
+        jnp.dot(h_all, part, preferred_element_type=F32).reshape(4, share, width)
+        for part in (w_q, w_k, w_v)
+    ]
+    grad_parts, qkv = lax.optimization_barrier((grad_parts, qkv))
+    mixed, queries, keys, values = attend_forward(me_arg, qkv, tables)
     middle = block_in + collect(
         lambda r: jnp.dot(mixed[r], w_out, preferred_element_type=F32)
     )
     normed_two, factor_two = normalize(middle)
     h2_parts = spread((normed_two * gain_two).astype(BF16))
-    h2_all = jnp.concatenate(h2_parts, axis=0)
-    gate_vals = jnp.dot(h2_all, w_gate, preferred_element_type=F32)
-    up_values = jnp.dot(h2_all, w_up, preferred_element_type=F32)
-    hidden = (jax.nn.gelu(gate_vals, approximate=False) * up_values).astype(BF16)
-
-    def quarter_of(tensor, r):
-        return lax.slice_in_dim(tensor, r * share, (r + 1) * share, axis=0)
-
-    final_rows = middle + collect(
-        lambda r: jnp.dot(quarter_of(hidden, r), w_down, preferred_element_type=F32)
-    )
-    activations = final_rows.astype(BF16)
-
-    down_share = scatter_columns(dot_tn(hidden, grad_all))
-    grad_hidden = dot_nt(grad_all, w_down)
 
     def product(gate_in, up_in):
         return jax.nn.gelu(gate_in, approximate=False) * up_in
 
-    _, pullback = jax.vjp(product, gate_vals, up_values)
-    grad_gate, grad_up = (item.astype(BF16) for item in pullback(grad_hidden))
+    halves = []
+    for start in (0, 2):
+        h_rows = jnp.concatenate(h2_parts[start : start + 2], axis=0)
+        g_rows = jnp.concatenate(grad_parts[start : start + 2], axis=0)
+        gate_vals = jnp.dot(h_rows, w_gate, preferred_element_type=F32)
+        up_values = jnp.dot(h_rows, w_up, preferred_element_type=F32)
+        value, pullback = jax.vjp(product, gate_vals, up_values)
+        grad_gate, grad_up = pullback(dot_nt(g_rows, w_down))
+        halves.append(
+            (h_rows, g_rows, value.astype(BF16), grad_gate.astype(BF16), grad_up.astype(BF16))
+        )
+
+    def quarter_of(part, r):
+        return halves[r // 2][part][(r % 2) * share : (r % 2 + 1) * share]
+
     grad_h_two = collect(
-        lambda r: dot_nt(quarter_of(grad_gate, r), w_gate) + dot_nt(quarter_of(grad_up, r), w_up)
+        lambda r: dot_nt(quarter_of(3, r), w_gate) + dot_nt(quarter_of(4, r), w_up)
+    )
+    h2_all, grad_all, hidden, grad_gate, grad_up = [
+        jnp.concatenate(pair, axis=0) for pair in zip(*halves)
+    ]
+    down_share = scatter_columns(dot_tn(hidden, grad_all))
+    in_share = jnp.stack(
+        [scatter_rows(dot_tn(h2_all, grad_gate)), scatter_rows(dot_tn(h2_all, grad_up))], axis=1
     )
     grad_norm_two, gain_two_grad = norm_back(grad_h_two, normed_two, factor_two, gain_two)
     grad_middle = grad_final + grad_norm_two
-    grad_mid_all = jnp.concatenate(spread(grad_middle.astype(BF16)), axis=0)
-    in_share = scatter_rows(
-        jnp.concatenate([dot_tn(h2_all, grad_gate), dot_tn(h2_all, grad_up)], axis=1)
-    ).reshape(-1, 2, units)
+    grad_mid_own, late_hidden = lax.optimization_barrier(
+        (grad_middle.astype(BF16), [item[2] for item in halves])
+    )
+    grad_mid_all = jnp.concatenate(spread(grad_mid_own), axis=0)
+    activations = (
+        middle
+        + collect(
+            lambda r: jnp.dot(
+                late_hidden[r // 2][(r % 2) * share : (r % 2 + 1) * share],
+                w_down,
+                preferred_element_type=F32,
+            )
+        )
+    ).astype(BF16)
     grad_mixed = dot_nt(grad_mid_all, w_out).astype(BF16).reshape(4, share, width)
     grad_qkv = attend_backward(me_arg, queries, keys, values, grad_mixed, tables)
     out_share = scatter_columns(dot_tn(mixed.reshape(group_rows, width), grad_mid_all))
     grad_h_one = collect(lambda r: dot_nt(grad_qkv[r], w_qkv))
     grad_norm_one, gain_one_grad = norm_back(grad_h_one, normed_one, factor_one, gain_one)
     input_grad = (grad_middle + grad_norm_one).astype(BF16)
-    qkv_share = scatter_rows(dot_tn(h_all, grad_qkv.reshape(group_rows, 3 * width))).reshape(
-        -1, 3, width
-    )
-    gain_total = lax.psum(jnp.stack([gain_one_grad, gain_two_grad]), ("dp", "mp"))
-    own = attn_gain.shape[0]
-    gain_total = lax.dynamic_slice_in_dim(gain_total, lax.axis_index("dp") * own, own, 1)
+    flat_grad = grad_qkv.reshape(group_rows, 3 * width)
+    qkv_share = jnp.stack(
+        [
+            scatter_rows(dot_tn(h_all, flat_grad[:, part * width : (part + 1) * width]))
+            for part in range(3)
+        ],
+        axis=1,
+    )
+    gain_total = jnp.stack([gain_one_grad, gain_two_grad]).reshape(2, lax.axis_size("dp"), -1)
+    gain_total = halving(jnp.transpose(gain_total, (1, 0, 2)))
+    for bit in (1, 2):
+        gain_total = gain_total + swap(gain_total, bit)
     return (
         activations,
         input_grad,

time: 495 us -> 451 us (0.911)
  blocking collectives: 92.6 us -> 0 us
  starting transfers between devices: 16.8 us -> 81.1 us
  waiting for transfers between devices: 202 us -> 173 us
  local copies, waits for them, and re-layouts: 22 us -> 44.1 us
  other arithmetic: 29.4 us -> 47.4 us
  matrix products: 82.7 us -> 68.8 us
  between operations: 15.4 us -> 2.64 us
    ppermute x0 -> x48, waiting for transfers between devices: none -> 141 us  [the longest x24 78.9 us: halving(): arrived = lax.ppermute(away, 'dp', pairs(bits[step]))]
    reduce_scatter x3 -> x0, waiting for transfers between devices: 73.1 us -> none  [the longest x1 65.7 us: scatter_rows(): lax.psum_scatter(grad.astype(BF16), 'dp', scatter_dimension=0, tiled=True)]
    ppermute x27 -> x29, waiting for transfers between devices: 103 us -> 32.3 us  [swap(): return lax.ppermute(tensor, 'mp', [(i, i ^ bit) for i in range(4)])]
    ppermute x0 -> x48, starting transfers between devices: none -> 66.6 us  [the longest x24 38.6 us: doubling(): other = lax.ppermute(held, 'dp', pairs(bit))]
    all_gather x2 -> x0, blocking collectives: 52.7 us -> none  [the longest x1 32.1 us: gather_columns(): parts = lax.all_gather(shard, 'dp', axis=0)]
    psum x1 -> x0, blocking collectives: 39.9 us -> none  [body(): lax.psum(jnp.stack([gain_one_grad, gain_two_grad]), ('dp', 'mp'))]
    another operation x1 -> x10, local copies, waits for them, and re-layouts: 0.11 us -> 26 us  [the longest x2 9.3 us: halving(): held = parts.reshape((2,) * len(bits) + parts.shape[1:])]
    unnamed x8 -> x0, waiting for transfers between devices: 23.3 us -> none
  transfers between devices with their start and end apart: 34 -> 77, of which waited for: 12 -> 37; matrix products, arithmetic and copies ran while one was open for 20% -> 35% of each run, Pallas kernels for 5% -> 6%
where the time goes in v2:
time: 451 us; the launch traced here: 443 us
  waiting for transfers between devices  173 us (38%)
  starting transfers between devices  81.1 us (18%)
  matrix products  68.8 us (15%)
  other arithmetic  47.4 us (11%)
  local copies, waits for them, and re-layouts  44.1 us (10%)
  Pallas kernels  25.7 us (6%)
    ppermute x24, waiting for transfers between devices, halving(): arrived = lax.ppermute(away, 'dp', pairs(bits[step]))  78.9 us
    ppermute x24, waiting for transfers between devices, doubling(): other = lax.ppermute(held, 'dp', pairs(bit))  61.8 us
    ppermute x24, starting transfers between devices, doubling(): other = lax.ppermute(held, 'dp', pairs(bit))  38.6 us
    ppermute x29, waiting for transfers between devices, swap(): return lax.ppermute(tensor, 'mp', [(i, i ^ bit) for i in range(4)])  32.3 us
    ppermute x24, starting transfers between devices, halving(): arrived = lax.ppermute(away, 'dp', pairs(bits[step]))  28 us
    dot_general x15, matrix products, dot_nt(): lax.dot_general(left, right, (((1,), (1,)), ((), ())), preferred_element_...  23.3 us
    dot_general x7, matrix products, dot_tn(): lax.dot_general(left, right, (((0,), (0,)), ((), ())), preferred_element_...  18.5 us
    pallas_call x1, Pallas kernels, attend_backward(): pl.pallas_call(backward_kernel, out_shape=jax.ShapeDtypeStruct((quarters,...  14.8 us
  transfers between devices with their start and end apart: 77, of which 37 were waited for; matrix products, arithmetic and copies ran while one was open for 35% of the time, Pallas kernels for 6%

profile of v2, /device:TPU:0, one launch (start us, length us, event | category | flops | bytes accessed | tf_op | source)
XLA Modules:
  0.0 442.8 jit_solution(2065349698753364638)
XLA Ops:
  53.6 5.7 %collective-permute-done.28 = bf16[128,656]{0,1:T(8,128)(2,1)S(1)} collective-permute-done((bf16[128,656]{0,1:T(8,128)(2,1)S(1)}, bf16[128,656]{0,1:T(8,128)(2,1)S(1)}, u32[]{:S(2)}, u32[]{:S(2)}) %collective-permute-start.28) | collective-permute-done | bytes 167968 | tf_op jit(solution)/shard_map/ppermute | solution.py:291
  60.0 5.6 %collective-permute-done.34 = bf16[128,656]{0,1:T(8,128)(2,1)S(1)} collective-permute-done((bf16[128,656]{0,1:T(8,128)(2,1)S(1)}, bf16[128,656]{0,1:T(8,128)(2,1)S(1)}, u32[]{:S(2)}, u32[]{:S(2)}) %collective-permute-start.34) | collective-permute-done | bytes 167968 | tf_op jit(solution)/shard_map/ppermute | solution.py:291
  68.0 7.4 %collective-permute-done.31 = bf16[656,128]{1,0:T(8,128)(2,1)S(1)} collective-permute-done((bf16[656,128]{1,0:T(8,128)(2,1)S(1)}, bf16[656,128]{1,0:T(8,128)(2,1)S(1)}, u32[]{:S(2)}, u32[]{:S(2)}) %collective-permute-start.31) | collective-permute-done | bytes 167968 | tf_op jit(solution)/shard_map/ppermute | solution.py:291
  75.4 5.8 %collective-permute-start.22 = (bf16[2,256,128]{2,1,0:T(8,128)(2,1)S(1)}, bf16[2,256,128]{2,1,0:T(8,128)(2,1)S(1)}, u32[]{:S(2)}, u32[]{:S(2)}) collective-permute-start(bf16[2,256,128]{2,1,0:T(8,128)(2,1)S(1)} %pad_maximum_fusion.32), channel_id=1, source_target_pairs={{0,8},{4,12},{8,0},{12,4},{16,24},{20,28},{24,16},{28,20},{1,9},{5... | collective-permute-start | bytes 393224 | tf_op jit(solution)/shard_map/ppermute | solution.py:291
  86.4 4.1 collective-permute-done.14
  114.5 4.4 fusion.2
  118.9 4.0 fusion.4
  127.4 10.9 %attend_forward.1 = (bf16[4,384,256]{2,1,0:T(8,128)(2,1)S(1)}, bf16[1536,256]{1,0:T(8,128)(2,1)S(1)}, bf16[1664,256]{1,0:T(8,128)(2,1)S(1)}, bf16[1664,256]{1,0:T(8,128)(2,1)S(1)}) custom-call(s32[1]{0:T(128)} %bitcast.me_ref, f32[4,384,256]{2,1,0:T(8,128)S(1)} %fusion.172.qi_ref, f32[4,384,256]{2,1,0:T(8,128)S(1)} %fusion.173.ki_ref, ...), custom_call_target="tpu_custom_call" | custom-call | flops 805306368 | bytes 6291456 | tf_op jit(solution)/shard_map/attend_forward/pallas_call | solution.py:209
  150.4 4.7 %reshape_reshape.33 = bf16[1024,656]{0,1:T(8,128)(2,1)} reshape(bf16[2,2,2,128,656]{3,2,1,0,4:T(2,128)(2,1)} %copy.119) | data formatting | bytes 2686976 | tf_op jit(solution)/shard_map/reshape;reshape | solution.py:318
  155.2 17.0 %collective-permute-done.36 = bf16[2,2,128,656]{2,3,0,1:T(8,128)(2,1)} collective-permute-done((bf16[2,2,128,656]{2,3,0,1:T(8,128)(2,1)}, bf16[2,2,128,656]{2,3,0,1:T(8,128)(2,1)}, u32[]{:S(2)}, u32[]{:S(2)}) %collective-permute-start.36) | collective-permute-done | bytes 671776 | tf_op jit(solution)/shard_map/ppermute | solution.py:291
  182.0 4.4 reshape_reshape.34
  192.3 6.8 %multiply_convert_fusion.1 = (bf16[768,656]{0,1:T(8,128)(2,1)S(1)}, f32[768,656]{0,1:T(8,128)S(1)}, f32[768,656]{0,1:T(8,128)S(1)}) fusion(f32[768,656]{0,1:T(8,128)S(1)} %fusion.88, bf16[1024,656]{0,1:T(8,128)(2,1)S(1)} %copy-done.38, bf16[384,1024]{1,0:T(8,128)(2,1)} %collective-permute-done.27, bf16[384,1024]{1,0:T(8,128)(2,1)} %multiply_convert_fusion.4), kind=kOutput, calls=%fused_computation.38 | convolution fusion | flops 1068195840 | bytes 9969664 | tf_op jit(solution)/shard_map/dot_general | solution.py:403
  199.1 3.7 multiply_convert_fusion.3
  203.6 4.5 %collective-permute-done.38 = bf16[384,1024]{1,0:T(8,128)(2,1)S(1)} collective-permute-done((bf16[384,1024]{1,0:T(8,128)(2,1)}, bf16[384,1024]{1,0:T(8,128)(2,1)S(1)}, u32[]{:S(2)}, u32[]{:S(2)}) %collective-permute-start.38) | collective-permute-done | bytes 786464 | tf_op jit(solution)/shard_map/ppermute | solution.py:246
  215.8 5.6 %multiply_convert_fusion = (bf16[768,656]{0,1:T(8,128)(2,1)S(1)}, f32[768,656]{0,1:T(8,128)S(1)}, f32[768,656]{0,1:T(8,128)S(1)}) fusion(f32[768,656]{0,1:T(8,128)S(1)} %fusion.175, bf16[768,1024]{1,0:T(8,128)(2,1)S(1)} %constant_dynamic-update-slice_fusion, bf16[1024,656]{0,1:T(8,128)(2,1)S(1)} %copy-done.38), kind=kOutput, calls=%fused_computation.37 | convolution fusion | flops 1065050112 | bytes 9969664 | tf_op jit(solution)/shard_map/dot_general | solution.py:403
  227.7 3.9 fusion.68
  232.9 4.7 %fusion.44 = bf16[1024,656]{0,1:T(8,128)(2,1)} fusion(bf16[768,656]{0,1:T(8,128)(2,1)S(1)} %get-tuple-element.65, bf16[768,656]{0,1:T(8,128)(2,1)S(1)} %get-tuple-element.63, bf16[384,1024]{1,0:T(8,128)(2,1)S(1)} %collective-permute-done.39, bf16[384,1024]{1,0:T(8,128)(2,1)S(1)} %collective-permute-done.38, bf16[384,1024]{1,0:T(8,128)(2,1)} %collective-permute-done.27, ...), kind=kOutput, calls=%fused_computation.77 | convolution fusion | flops 2080882688 | bytes 6504448 | tf_op jit(solution)/shard_map/dot_general | solution.py:265
  237.6 4.5 %reshape_reshape.38 = bf16[2,2,2,128,656]{3,2,1,0,4:T(2,128)(2,1)} reshape(bf16[1024,656]{0,1:T(8,128)(2,1)} %fusion.44) | data formatting | bytes 2686976 | tf_op jit(solution)/shard_map/reshape;reshape | solution.py:305
  242.1 5.8 %fusion.41 = bf16[1024,656]{0,1:T(8,128)(2,1)} fusion(bf16[768,656]{0,1:T(8,128)(2,1)} %copy-done.64, bf16[768,656]{0,1:T(8,128)(2,1)} %copy-done.66, bf16[384,1024]{1,0:T(8,128)(2,1)} %copy-done.41, bf16[384,1024]{1,0:T(8,128)(2,1)} %copy-done.40, bf16[384,1024]{1,0:T(8,128)(2,1)} %collective-permute-done.27, bf16[384,1024]{1,0:T(8,128)(2,1)} %multiply_convert_fusion.4), kind=kOutput, calls=%fused_computation.76 | convolution fusion | flops 2080882688 | bytes 6504448 | tf_op jit(solution)/shard_map/dot_general | solution.py:265
  247.8 4.8 %reshape_reshape.39 = bf16[2,2,2,128,656]{3,2,1,0,4:T(2,128)(2,1)} reshape(bf16[1024,656]{0,1:T(8,128)(2,1)} %fusion.41) | data formatting | bytes 2686976 | tf_op jit(solution)/shard_map/reshape;reshape | solution.py:305
  263.9 8.0 %collective-permute-done.74 = bf16[2,2,656,128]{3,2,1,0:T(8,128)(2,1)S(1)} collective-permute-done((bf16[2,2,656,128]{3,2,1,0:T(8,128)(2,1)S(1)}, bf16[2,2,656,128]{3,2,1,0:T(8,128)(2,1)S(1)}, u32[]{:S(2)}, u32[]{:S(2)}) %collective-permute-start.74) | collective-permute-done | bytes 671776 | tf_op jit(solution)/shard_map/ppermute | solution.py:310
  273.9 12.4 %collective-permute-done.71 = bf16[2,2,128,656]{2,3,0,1:T(8,128)(2,1)S(1)} collective-permute-done((bf16[2,2,128,656]{2,3,0,1:T(8,128)(2,1)S(1)}, bf16[2,2,128,656]{2,3,0,1:T(8,128)(2,1)S(1)}, u32[]{:S(2)}, u32[]{:S(2)}) %collective-permute-start.71) | collective-permute-done | bytes 671776 | tf_op jit(solution)/shard_map/ppermute | solution.py:310
  288.3 12.0 %collective-permute-done.68 = bf16[2,2,128,656]{2,3,0,1:T(8,128)(2,1)S(1)} collective-permute-done((bf16[2,2,128,656]{2,3,0,1:T(8,128)(2,1)S(1)}, bf16[2,2,128,656]{2,3,0,1:T(8,128)(2,1)S(1)}, u32[]{:S(2)}, u32[]{:S(2)}) %collective-permute-start.68) | collective-permute-done | bytes 671776 | tf_op jit(solution)/shard_map/ppermute | solution.py:310
  309.2 4.3 collective-permute-done.69
  314.7 9.8 %collective-permute-done.76 = bf16[656,128]{1,0:T(8,128)(2,1)S(1)} collective-permute-done((bf16[656,128]{1,0:T(8,128)(2,1)S(1)}, bf16[656,128]{1,0:T(8,128)(2,1)S(1)}, u32[]{:S(2)}, u32[]{:S(2)}) %collective-permute-start.76) | collective-permute-done | bytes 167968 | tf_op jit(solution)/shard_map/ppermute | solution.py:310
  335.3 12.8 %collective-permute-done.46 = bf16[384,1024]{1,0:T(8,128)(2,1)S(1)} collective-permute-done((bf16[384,1024]{1,0:T(8,128)(2,1)S(1)}, bf16[384,1024]{1,0:T(8,128)(2,1)S(1)}, u32[]{:S(2)}, u32[]{:S(2)}) %collective-permute-start.46) | collective-permute-done | bytes 786464 | tf_op jit(solution)/shard_map/ppermute | solution.py:246
  352.8 14.8 %attend_backward.1 = bf16[4,384,768]{2,1,0:T(8,128)(2,1)S(1)} custom-call(s32[1]{0:T(128)} %bitcast.me_ref, bf16[1536,256]{1,0:T(8,128)(2,1)S(1)} %copy-done.3, bf16[1664,256]{1,0:T(8,128)(2,1)S(1)} %get-tuple-element.43.k_ref, bf16[1664,256]{1,0:T(8,128)(2,1)S(1)} %copy-done.1, bf16[4,384,256]{2,1,0:T(8,128)(2,1)S(1)} %bitcast.445, ...), custom_call_target="tpu_custom_call" | custom-call | flops 2013265920 | bytes 6291456 | tf_op jit(solution)/shard_map/attend_backward/pallas_call | solution.py:231
  381.3 5.5 %collective-permute-done.62 = bf16[2,2,128,256]{3,2,0,1:T(8,128)(2,1)S(1)} collective-permute-done((bf16[2,2,128,256]{3,2,0,1:T(8,128)(2,1)S(1)}, bf16[2,2,128,256]{3,2,0,1:T(8,128)(2,1)S(1)}, u32[]{:S(2)}, u32[]{:S(2)}) %collective-permute-start.62) | collective-permute-done | bytes 262176 | tf_op jit(solution)/shard_map/ppermute | solution.py:310
  386.9 5.5 %collective-permute-done.59 = bf16[2,2,128,256]{3,2,0,1:T(8,128)(2,1)S(1)} collective-permute-done((bf16[2,2,128,256]{3,2,0,1:T(8,128)(2,1)S(1)}, bf16[2,2,128,256]{3,2,0,1:T(8,128)(2,1)S(1)}, u32[]{:S(2)}, u32[]{:S(2)}) %collective-permute-start.59) | collective-permute-done | bytes 262176 | tf_op jit(solution)/shard_map/ppermute | solution.py:310
  392.5 4.6 %collective-permute-done.56 = bf16[2,2,128,256]{3,2,0,1:T(8,128)(2,1)S(1)} collective-permute-done((bf16[2,2,128,256]{3,2,0,1:T(8,128)(2,1)S(1)}, bf16[2,2,128,256]{3,2,0,1:T(8,128)(2,1)S(1)}, u32[]{:S(2)}, u32[]{:S(2)}) %collective-permute-start.56) | collective-permute-done | bytes 262176 | tf_op jit(solution)/shard_map/ppermute | solution.py:310
  400.3 3.9 collective-permute-done.60
  412.8 11.8 %collective-permute-done.50 = bf16[384,1024]{1,0:T(8,128)(2,1)S(1)} collective-permute-done((bf16[384,1024]{1,0:T(8,128)(2,1)S(1)}, bf16[384,1024]{1,0:T(8,128)(2,1)S(1)}, u32[]{:S(2)}, u32[]{:S(2)}) %collective-permute-start.50) | collective-permute-done | bytes 786464 | tf_op jit(solution)/shard_map/ppermute | solution.py:246
  (488 shorter events, 216.6 us)
Async XLA Ops:
  0.7 18.1 %collective-permute-start.19 = (s32[384]{0:T(512)}, s32[384]{0:T(512)S(1)}, u32[]{:S(2)}, u32[]{:S(2)}) collective-permute-start(s32[384]{0:T(512)} %param.10), channel_id=1, source_target_pairs={{0,2},{1,3},{2,0},{3,1},{4,6},{5,7},{6,4},{7,5},{8,10},{9,11},{10,... | collective-permute-start | bytes 4616 | tf_op jit(solution)/shard_map/ppermute | solution.py:246
  6.7 104.3 %collective-permute-start.1 = (bf16[384,1024]{1,0:T(8,128)(2,1)}, bf16[384,1024]{1,0:T(8,128)(2,1)}, u32[]{:S(2)}, u32[]{:S(2)}) collective-permute-start(bf16[384,1024]{1,0:T(8,128)(2,1)} %fusion.67), channel_id=1, source_target_pairs={{0,2},{1,3},{2,0},{3,1},{4,6},{5,7},{6,4},{7,5},{8,10},{9,11},{10,... | collective-permute-start | bytes 2359304 | tf_op jit(solution)/shard_map/ppermute | solution.py:246
  6.9 119.6 %collective-permute-start = (bf16[384,1024]{1,0:T(8,128)(2,1)}, bf16[384,1024]{1,0:T(8,128)(2,1)}, u32[]{:S(2)}, u32[]{:S(2)}) collective-permute-start(bf16[384,1024]{1,0:T(8,128)(2,1)} %fusion.67), channel_id=1, source_target_pairs={{0,1},{1,0},{2,3},{3,2},{4,5},{5,4},{6,7},{7,6},{8,9},{9,8},{10,11... | collective-permute-start | bytes 2359304 | tf_op jit(solution)/shard_map/ppermute | solution.py:246
  30.7 63.3 %collective-permute-start.4 = (bf16[384,1024]{1,0:T(8,128)(2,1)S(1)}, bf16[384,1024]{1,0:T(8,128)(2,1)}, u32[]{:S(2)}, u32[]{:S(2)}) collective-permute-start(bf16[384,1024]{1,0:T(8,128)(2,1)S(1)} %copy-done.8), channel_id=1, source_target_pairs={{0,2},{1,3},{2,0},{3,1},{4,6},{5,7},{6,4},{7,5},{8,10},{9,11},{10,... | collective-permute-start | bytes 2359304 | tf_op jit(solution)/shard_map/ppermute | solution.py:246
  43.2 41.5 %collective-permute-start.11 = (bf16[2,2,128,256]{3,2,0,1:T(8,128)(2,1)S(1)}, bf16[2,2,128,256]{3,2,0,1:T(8,128)(2,1)S(1)}, u32[]{:S(2)}, u32[]{:S(2)}) collective-permute-start(bf16[2,2,128,256]{3,2,0,1:T(8,128)(2,1)S(1)} %pad_maximum_fusion.25), channel_id=1, source_target_pairs={{0,4},{4,0},{8,12},{12,8},{16,20},{20,16},{24,28},{28,24},{1,5},{5... | collective-permute-start | bytes 786440 | tf_op jit(solution)/shard_map/ppermute | solution.py:291
  90.5 20.6 %collective-permute-start.3 = (bf16[384,1024]{1,0:T(8,128)(2,1)S(1)}, bf16[384,1024]{1,0:T(8,128)(2,1)}, u32[]{:S(2)}, u32[]{:S(2)}) collective-permute-start(bf16[384,1024]{1,0:T(8,128)(2,1)S(1)} %copy-done.8), channel_id=1, source_target_pairs={{0,1},{1,0},{2,3},{3,2},{4,5},{5,4},{6,7},{7,6},{8,9},{9,8},{10,11... | collective-permute-start | bytes 2359304 | tf_op jit(solution)/shard_map/ppermute | solution.py:246
  94.0 18.4 %collective-permute-start.5 = (bf16[384,1024]{1,0:T(8,128)(2,1)}, bf16[384,1024]{1,0:T(8,128)(2,1)}, u32[]{:S(2)}, u32[]{:S(2)}) collective-permute-start(bf16[384,1024]{1,0:T(8,128)(2,1)} %collective-permute-done.4), channel_id=1, source_target_pairs={{0,1},{1,0},{2,3},{3,2},{4,5},{5,4},{6,7},{7,6},{8,9},{9,8},{10,11... | collective-permute-start | bytes 2359304 | tf_op jit(solution)/shard_map/ppermute | solution.py:246
  107.7 31.5 %collective-permute-start.32 = (bf16[2,656,128]{2,1,0:T(8,128)(2,1)}, bf16[2,656,128]{2,1,0:T(8,128)(2,1)S(1)}, u32[]{:S(2)}, u32[]{:S(2)}) collective-permute-start(bf16[2,656,128]{2,1,0:T(8,128)(2,1)} %pad_maximum_fusion.23), channel_id=1, source_target_pairs={{0,8},{4,12},{8,0},{12,4},{16,24},{20,28},{24,16},{28,20},{1,9},{5... | collective-permute-start | bytes 1007624 | tf_op jit(solution)/shard_map/ppermute | solution.py:291
  111.0 30.2 %collective-permute-start.35 = (bf16[2,128,656]{1,2,0:T(8,128)(2,1)S(1)}, bf16[2,128,656]{1,2,0:T(8,128)(2,1)S(1)}, u32[]{:S(2)}, u32[]{:S(2)}) collective-permute-start(bf16[2,128,656]{1,2,0:T(8,128)(2,1)S(1)} %copy-done.52), channel_id=1, source_target_pairs={{0,8},{4,12},{8,0},{12,4},{16,24},{20,28},{24,16},{28,20},{1,9},{5... | collective-permute-start | bytes 1007624 | tf_op jit(solution)/shard_map/ppermute | solution.py:291
  111.1 36.6 %collective-permute-start.30 = (bf16[2,2,128,656]{2,3,0,1:T(8,128)(2,1)S(1)}, bf16[2,2,128,656]{2,3,0,1:T(8,128)(2,1)S(1)}, u32[]{:S(2)}, u32[]{:S(2)}) collective-permute-start(bf16[2,2,128,656]{2,3,0,1:T(8,128)(2,1)S(1)} %pad_maximum_fusion.11), channel_id=1, source_target_pairs={{0,4},{4,0},{8,12},{12,8},{16,20},{20,16},{24,28},{28,24},{1,5},{5... | collective-permute-start | bytes 2015240 | tf_op jit(solution)/shard_map/ppermute | solution.py:291
  140.4 46.0 %collective-permute-start.33 = (bf16[2,2,656,128]{3,2,1,0:T(8,128)(2,1)}, bf16[2,2,656,128]{3,2,1,0:T(8,128)(2,1)}, u32[]{:S(2)}, u32[]{:S(2)}) collective-permute-start(bf16[2,2,656,128]{3,2,1,0:T(8,128)(2,1)} %pad_maximum_fusion.12), channel_id=1, source_target_pairs={{0,4},{4,0},{8,12},{12,8},{16,20},{20,16},{24,28},{28,24},{1,5},{5... | collective-permute-start | bytes 2015240 | tf_op jit(solution)/shard_map/ppermute | solution.py:291
  142.3 29.9 %collective-permute-start.36 = (bf16[2,2,128,656]{2,3,0,1:T(8,128)(2,1)}, bf16[2,2,128,656]{2,3,0,1:T(8,128)(2,1)}, u32[]{:S(2)}, u32[]{:S(2)}) collective-permute-start(bf16[2,2,128,656]{2,3,0,1:T(8,128)(2,1)} %pad_maximum_fusion.13), channel_id=1, source_target_pairs={{0,4},{4,0},{8,12},{12,8},{16,20},{20,16},{24,28},{28,24},{1,5},{5... | collective-permute-start | bytes 2015240 | tf_op jit(solution)/shard_map/ppermute | solution.py:291
  144.9 30.1 %collective-permute-start.24 = (bf16[384,1024]{1,0:T(8,128)(2,1)}, bf16[384,1024]{1,0:T(8,128)(2,1)}, u32[]{:S(2)}, u32[]{:S(2)}) collective-permute-start(bf16[384,1024]{1,0:T(8,128)(2,1)} %convolution_convert_fusion.6), channel_id=1, source_target_pairs={{0,1},{1,0},{2,3},{3,2},{4,5},{5,4},{6,7},{7,6},{8,9},{9,8},{10,11... | collective-permute-start | bytes 2359304 | tf_op jit(solution)/shard_map/ppermute | solution.py:246
  146.2 28.8 %collective-permute-start.26 = (bf16[384,1024]{1,0:T(8,128)(2,1)}, bf16[384,1024]{1,0:T(8,128)(2,1)}, u32[]{:S(2)}, u32[]{:S(2)}) collective-permute-start(bf16[384,1024]{1,0:T(8,128)(2,1)} %add_convert_fusion.8), channel_id=1, source_target_pairs={{0,2},{1,3},{2,0},{3,1},{4,6},{5,7},{6,4},{7,5},{8,10},{9,11},{10,... | collective-permute-start | bytes 2359304 | tf_op jit(solution)/shard_map/ppermute | solution.py:246
  187.9 20.2 %collective-permute-start.38 = (bf16[384,1024]{1,0:T(8,128)(2,1)}, bf16[384,1024]{1,0:T(8,128)(2,1)S(1)}, u32[]{:S(2)}, u32[]{:S(2)}) collective-permute-start(bf16[384,1024]{1,0:T(8,128)(2,1)} %multiply_convert_fusion.4), channel_id=1, source_target_pairs={{0,2},{1,3},{2,0},{3,1},{4,6},{5,7},{6,4},{7,5},{8,10},{9,11},{10,... | collective-permute-start | bytes 2359304 | tf_op jit(solution)/shard_map/ppermute | solution.py:246
  209.9 118.3 %collective-permute-start.37 = (bf16[384,1024]{1,0:T(8,128)(2,1)}, bf16[384,1024]{1,0:T(8,128)(2,1)}, u32[]{:S(2)}, u32[]{:S(2)}) collective-permute-start(bf16[384,1024]{1,0:T(8,128)(2,1)} %add_convert_fusion.7), channel_id=1, source_target_pairs={{0,1},{1,0},{2,3},{3,2},{4,5},{5,4},{6,7},{7,6},{8,9},{9,8},{10,11... | collective-permute-start | bytes 2359304 | tf_op jit(solution)/shard_map/ppermute | solution.py:246
  227.7 74.6 %collective-permute-start.40 = (bf16[384,1024]{1,0:T(8,128)(2,1)}, bf16[384,1024]{1,0:T(8,128)(2,1)}, u32[]{:S(2)}, u32[]{:S(2)}) collective-permute-start(bf16[384,1024]{1,0:T(8,128)(2,1)} %add_convert_fusion.6), channel_id=1, source_target_pairs={{0,1},{1,0},{2,3},{3,2},{4,5},{5,4},{6,7},{7,6},{8,9},{9,8},{10,11... | collective-permute-start | bytes 2359304 | tf_op jit(solution)/shard_map/ppermute | solution.py:246
  254.0 17.9 %collective-permute-start.74 = (bf16[2,2,656,128]{3,2,1,0:T(8,128)(2,1)S(1)}, bf16[2,2,656,128]{3,2,1,0:T(8,128)(2,1)S(1)}, u32[]{:S(2)}, u32[]{:S(2)}) collective-permute-start(bf16[2,2,656,128]{3,2,1,0:T(8,128)(2,1)S(1)} %dynamic-slice_bitcast_fusion), channel_id=1, source_target_pairs={{0,4},{4,0},{8,12},{12,8},{16,20},{20,16},{24,28},{28,24},{1,5},{5... | collective-permute-start | bytes 2015240 | tf_op jit(solution)/shard_map/ppermute | solution.py:310
  257.7 28.6 %collective-permute-start.71 = (bf16[2,2,128,656]{2,3,0,1:T(8,128)(2,1)S(1)}, bf16[2,2,128,656]{2,3,0,1:T(8,128)(2,1)S(1)}, u32[]{:S(2)}, u32[]{:S(2)}) collective-permute-start(bf16[2,2,128,656]{2,3,0,1:T(8,128)(2,1)S(1)} %bitcast.467), channel_id=1, source_target_pairs={{0,4},{4,0},{8,12},{12,8},{16,20},{20,16},{24,28},{28,24},{1,5},{5... | collective-permute-start | bytes 2015240 | tf_op jit(solution)/shard_map/ppermute | solution.py:310
  262.0 38.4 %collective-permute-start.68 = (bf16[2,2,128,656]{2,3,0,1:T(8,128)(2,1)S(1)}, bf16[2,2,128,656]{2,3,0,1:T(8,128)(2,1)S(1)}, u32[]{:S(2)}, u32[]{:S(2)}) collective-permute-start(bf16[2,2,128,656]{2,3,0,1:T(8,128)(2,1)S(1)} %bitcast.466), channel_id=1, source_target_pairs={{0,4},{4,0},{8,12},{12,8},{16,20},{20,16},{24,28},{28,24},{1,5},{5... | collective-permute-start | bytes 2015240 | tf_op jit(solution)/shard_map/ppermute | solution.py:310
  272.1 33.7 %collective-permute-start.75 = (bf16[2,656,128]{2,1,0:T(8,128)(2,1)S(1)}, bf16[2,656,128]{2,1,0:T(8,128)(2,1)S(1)}, u32[]{:S(2)}, u32[]{:S(2)}) collective-permute-start(bf16[2,656,128]{2,1,0:T(8,128)(2,1)S(1)} %dynamic-slice_bitcast_fusion.1), channel_id=1, source_target_pairs={{0,8},{4,12},{8,0},{12,4},{16,24},{20,28},{24,16},{28,20},{1,9},{5... | collective-permute-start | bytes 1007624 | tf_op jit(solution)/shard_map/ppermute | solution.py:310
  286.5 22.2 %collective-permute-start.72 = (bf16[2,128,656]{1,2,0:T(8,128)(2,1)S(1)}, bf16[2,128,656]{1,2,0:T(8,128)(2,1)S(1)}, u32[]{:S(2)}, u32[]{:S(2)}) collective-permute-start(bf16[2,128,656]{1,2,0:T(8,128)(2,1)S(1)} %dynamic-slice_bitcast_fusion.2), channel_id=1, source_target_pairs={{0,8},{4,12},{8,0},{12,4},{16,24},{20,28},{24,16},{28,20},{1,9},{5... | collective-permute-start | bytes 1007624 | tf_op jit(solution)/shard_map/ppermute | solution.py:310
  304.3 23.9 %collective-permute-start.41 = (bf16[384,1024]{1,0:T(8,128)(2,1)S(1)}, bf16[384,1024]{1,0:T(8,128)(2,1)S(1)}, u32[]{:S(2)}, u32[]{:S(2)}) collective-permute-start(bf16[384,1024]{1,0:T(8,128)(2,1)S(1)} %add_convert_fusion.5), channel_id=1, source_target_pairs={{0,2},{1,3},{2,0},{3,1},{4,6},{5,7},{6,4},{7,5},{8,10},{9,11},{10,... | collective-permute-start | bytes 2359304 | tf_op jit(solution)/shard_map/ppermute | solution.py:246
  306.0 18.5 %collective-permute-start.76 = (bf16[656,128]{1,0:T(8,128)(2,1)S(1)}, bf16[656,128]{1,0:T(8,128)(2,1)S(1)}, u32[]{:S(2)}, u32[]{:S(2)}) collective-permute-start(bf16[656,128]{1,0:T(8,128)(2,1)S(1)} %dynamic-slice_bitcast_fusion.5), channel_id=1, source_target_pairs={{0,16},{4,20},{8,24},{12,28},{16,0},{20,4},{24,8},{28,12},{1,17},{... | collective-permute-start | bytes 503816 | tf_op jit(solution)/shard_map/ppermute | solution.py:310
  308.9 19.3 %collective-permute-start.73 = (bf16[128,656]{0,1:T(8,128)(2,1)S(1)}, bf16[128,656]{0,1:T(8,128)(2,1)S(1)}, u32[]{:S(2)}, u32[]{:S(2)}) collective-permute-start(bf16[128,656]{0,1:T(8,128)(2,1)S(1)} %dynamic-slice_bitcast_fusion.6), channel_id=1, source_target_pairs={{0,16},{4,20},{8,24},{12,28},{16,0},{20,4},{24,8},{28,12},{1,17},{... | collective-permute-start | bytes 503816 | tf_op jit(solution)/shard_map/ppermute | solution.py:310
  313.6 17.9 %collective-permute-start.70 = (bf16[128,656]{0,1:T(8,128)(2,1)S(1)}, bf16[128,656]{0,1:T(8,128)(2,1)S(1)}, u32[]{:S(2)}, u32[]{:S(2)}) collective-permute-start(bf16[128,656]{0,1:T(8,128)(2,1)S(1)} %dynamic-slice_bitcast_fusion.7), channel_id=1, source_target_pairs={{0,16},{4,20},{8,24},{12,28},{16,0},{20,4},{24,8},{28,12},{1,17},{... | collective-permute-start | bytes 503816 | tf_op jit(solution)/shard_map/ppermute | solution.py:310
  348.9 28.3 %collective-permute-start.42 = (bf16[384,1024]{1,0:T(8,128)(2,1)S(1)}, bf16[384,1024]{1,0:T(8,128)(2,1)S(1)}, u32[]{:S(2)}, u32[]{:S(2)}) collective-permute-start(bf16[384,1024]{1,0:T(8,128)(2,1)S(1)} %convolution_convert_fusion.4), channel_id=1, source_target_pairs={{0,1},{1,0},{2,3},{3,2},{4,5},{5,4},{6,7},{7,6},{8,9},{9,8},{10,11... | collective-permute-start | bytes 2359304 | tf_op jit(solution)/shard_map/ppermute | solution.py:246
  350.3 27.8 %collective-permute-start.44 = (bf16[384,1024]{1,0:T(8,128)(2,1)S(1)}, bf16[384,1024]{1,0:T(8,128)(2,1)S(1)}, u32[]{:S(2)}, u32[]{:S(2)}) collective-permute-start(bf16[384,1024]{1,0:T(8,128)(2,1)S(1)} %add_convert_fusion.4), channel_id=1, source_target_pairs={{0,2},{1,3},{2,0},{3,1},{4,6},{5,7},{6,4},{7,5},{8,10},{9,11},{10,... | collective-permute-start | bytes 2359304 | tf_op jit(solution)/shard_map/ppermute | solution.py:246
  374.4 18.1 %collective-permute-start.59 = (bf16[2,2,128,256]{3,2,0,1:T(8,128)(2,1)S(1)}, bf16[2,2,128,256]{3,2,0,1:T(8,128)(2,1)S(1)}, u32[]{:S(2)}, u32[]{:S(2)}) collective-permute-start(bf16[2,2,128,256]{3,2,0,1:T(8,128)(2,1)S(1)} %bitcast.488), channel_id=1, source_target_pairs={{0,4},{4,0},{8,12},{12,8},{16,20},{20,16},{24,28},{28,24},{1,5},{5... | collective-permute-start | bytes 786440 | tf_op jit(solution)/shard_map/ppermute | solution.py:310
  377.2 19.9 %collective-permute-start.56 = (bf16[2,2,128,256]{3,2,0,1:T(8,128)(2,1)S(1)}, bf16[2,2,128,256]{3,2,0,1:T(8,128)(2,1)S(1)}, u32[]{:S(2)}, u32[]{:S(2)}) collective-permute-start(bf16[2,2,128,256]{3,2,0,1:T(8,128)(2,1)S(1)} %bitcast.486), channel_id=1, source_target_pairs={{0,4},{4,0},{8,12},{12,8},{16,20},{20,16},{24,28},{28,24},{1,5},{5... | collective-permute-start | bytes 786440 | tf_op jit(solution)/shard_map/ppermute | solution.py:310
  378.2 34.7 %collective-permute-start.48 = (bf16[384,1024]{1,0:T(8,128)(2,1)S(1)}, bf16[384,1024]{1,0:T(8,128)(2,1)S(1)}, u32[]{:S(2)}, u32[]{:S(2)}) collective-permute-start(bf16[384,1024]{1,0:T(8,128)(2,1)S(1)} %convolution_convert_fusion.2), channel_id=1, source_target_pairs={{0,1},{1,0},{2,3},{3,2},{4,5},{5,4},{6,7},{7,6},{8,9},{9,8},{10,11... | collective-permute-start | bytes 2359304 | tf_op jit(solution)/shard_map/ppermute | solution.py:246
  381.2 26.1 %collective-permute-start.49 = (bf16[384,1024]{1,0:T(8,128)(2,1)S(1)}, bf16[384,1024]{1,0:T(8,128)(2,1)S(1)}, u32[]{:S(2)}, u32[]{:S(2)}) collective-permute-start(bf16[384,1024]{1,0:T(8,128)(2,1)S(1)} %convolution_convert_fusion.1), channel_id=1, source_target_pairs={{0,1},{1,0},{2,3},{3,2},{4,5},{5,4},{6,7},{7,6},{8,9},{9,8},{10,11... | collective-permute-start | bytes 2359304 | tf_op jit(solution)/shard_map/ppermute | solution.py:246
  (118 other events, 1182.8 us)
